TPU v7x, 32 devices: a whole 2x2x4 slice. The times are simulated.
32 devices in a mesh: blk: 4 (over x, core), grp: 8 (over z, y).
Axes of the slice: x: 2, y: 2, z: 4, core: 2. Of those that a mesh axis runs over, the one named last changes fastest.
Arguments:
- table: bfloat16 [65536, 512], P(('blk', 'grp')), may hold values from -6 to 6
- row_ids: int32 [4096], P(('blk', 'grp')), may hold values from 0 to 2047
- potentials: bfloat16 [4096], P(('blk', 'grp')), may hold values from -1 to 6
- centroids: bfloat16 [65536, 512], P(('blk', 'grp')), may hold values from -30 to 30
- balance: float32 [65536], P(('blk', 'grp')), may hold values from 0.001 to 1
Outputs:
- new_centroids: float32 [65536, 512], P(('blk', 'grp'))
- column_potential: float32 [65536], P(('blk', 'grp'))
Inputs may be any that keep to these rules, and one draw needn't show every extreme that they name: `row_ids`: offsets into the records held by the row's own device.
All inputs are finite; a program needn't handle non-finite values.
Results may differ from a plain program's by a relative error of at most 0.0027.
Values may be sent and summed in bfloat16 or wider, within the bound.
No kernel may reach another device: no remote copies, remote signals or barrier semaphores. Data moves between devices by JAX's collectives and lax.ppermute only.
A program may use at most 128 MiB of HBM per device.

v0:
```python
import math

import jax
import jax.numpy as jnp
from jax import lax
from jax.sharding import PartitionSpec as P


def shifted(block, axis, distance):
    devices = range(lax.axis_size(axis))
    route = [((i - distance) % len(devices), i) for i in devices]
    return lax.ppermute(block, axis, route)


def column_scores(rows, pots, norms, panel, scale):
    inner = lax.dot_general(
        rows, panel, (((1,), (1,)), ((), ())), preferred_element_type=jnp.float32
    )
    centre = jnp.sum(jnp.square(panel.astype(jnp.float32)), axis=1)
    cost = (norms[:, None] - 2.0 * inner + centre[None, :]) / rows.shape[1]
    return scale * (pots.astype(jnp.float32)[:, None] - cost)


def row_norms(rows):
    return jnp.sum(jnp.square(rows.astype(jnp.float32)), axis=1)


def visit(state, rows, pots, norms, panel, scale):
    peak, mass, numer = state
    scores = column_scores(rows, pots, norms, panel, scale)
    top = jnp.maximum(peak, jnp.max(scores, axis=0))
    shrink = jnp.exp(peak - top)
    expd = jnp.exp(scores - top[None, :])
    mass = mass * shrink + jnp.sum(expd, axis=0)
    weights = expd.astype(jnp.bfloat16)
    numer = numer * shrink[:, None] + lax.dot_general(
        weights, rows, (((0,), (0,)), ((), ())), preferred_element_type=jnp.float32
    )
    return (top, mass, numer)


def start_state(count, width):
    return (
        jnp.full((count,), -jnp.inf, jnp.float32),
        jnp.zeros((count,), jnp.float32),
        jnp.zeros((count, width), jnp.float32),
    )


def group_gather(local_rows, potentials):
    return (
        lax.all_gather(local_rows, "grp", axis=0, tiled=True),
        lax.all_gather(potentials, "grp", axis=0, tiled=True),
    )


def finish(state, target, scale):
    peak, mass, numer = state
    means = numer / mass[:, None]
    potential = (jnp.log(target) - peak - jnp.log(mass)) / scale
    return (means, potential)


def body(table, row_ids, potentials, centroids, balance):
    width = table.shape[1]
    scale = 1.5 * math.sqrt(width)
    local_rows = table[row_ids]
    count = centroids.shape[0]
    turns = lax.axis_size("blk")
    gathered, group_pots = group_gather(local_rows, potentials)
    norms = row_norms(gathered)
    state = start_state(count, width)
    panel = centroids
    for turn in range(turns):
        state = visit(state, gathered, group_pots, norms, panel, scale)
        if turn + 1 < turns:
            panel = shifted(panel, "blk", 1)
        state = shifted((state[0], state[1], state[2]), "blk", 1)
    return finish(state, balance, scale)


def solution(mesh):
    placed = (
        P(("blk", "grp"), None),
        P(("blk", "grp")),
        P(("blk", "grp")),
        P(("blk", "grp"), None),
        P(("blk", "grp")),
    )
    return jax.shard_map(
        body,
        mesh=mesh,
        in_specs=placed,
        out_specs=(P(("blk", "grp"), None), P(("blk", "grp"))),
        check_vma=False,
    )
```

profile of v0, /device:TPU:0, one launch (start us, length us, event | category | flops | bytes accessed | tf_op | source)
XLA Modules:
  0.0 320.7 jit_solution(3927552728120395934)
XLA Ops:
  7.2 0.0 copy-start
  7.2 0.0 all-gather.4.cloned.1.call-start
  7.2 0.5 collective-permute-start.2
  7.7 0.7 compare_select_fusion
  8.5 0.3 copy-done
  8.8 1.5 gather_fusion
  10.3 0.0 all-gather.4.cloned.1.call-update
  10.3 23.4 %collective-permute-done.2 = bf16[2048,512]{1,0:T(8,128)(2,1)} collective-permute-done((bf16[2048,512]{1,0:T(8,128)(2,1)}, bf16[2048,512]{1,0:T(8,128)(2,1)}, u32[]{:S(2)}, u32[]{:S(2)}) %collective-permute-start.2) | collective-permute-done | bytes 2097184 | tf_op jit(solution)/shard_map/ppermute | solution.py:12
  33.7 21.7 %all-gather.1 = bf16[8,1,128]{2,1,0:T(2,128)(2,1)S(1)} all-gather(bf16[1,1,128]{2,1,0:T(2,128)(2,1)} %bitcast.20), channel_id=1, replica_groups=mesh['blk'=4,'grp'=8] {'grp'}, dimensions={0}, use_global_device_ids=true | all-gather | bytes 2304 | tf_op jit(solution)/shard_map/all_gather | solution.py:53
  55.4 2.1 multiply_reduce_fusion.3
  57.5 0.0 all-gather.4.cloned.1.call-done
  57.5 1.5 multiply_reduce_fusion.4
  59.0 4.7 %fusion.33 = (f32[2048]{0:T(1024)S(1)}, f32[1024,2048]{1,0:T(8,128)S(1)}) fusion(f32[2048]{0:T(1024)S(1)} %multiply_reduce_fusion.3, bf16[1024,512]{1,0:T(8,128)(2,1)} %all-gather.4.cloned.1.call-done, bf16[2048,512]{1,0:T(8,128)(2,1)} %param.8, f32[1024]{0:T(1024)S(1)} %multiply_reduce_fusion.4, f32[1024]{0:T(1024)S(1)} %bitcast.14), kind=kOutput, calls=%fused_computation.49 | convolution fusion | flops 2162161664 | bytes 11558912 | tf_op jit(solution)/shard_map/dot_general | solution.py:16
  63.8 0.1 collective-permute-start.1
  63.9 1.2 fusion
  65.1 1.6 collective-permute-start.8
  66.7 4.5 %fusion.20 = f32[2048,512]{1,0:T(8,128)} fusion(bf16[1024,512]{1,0:T(8,128)(2,1)S(1)} %copy-done.2, f32[1024,2048]{1,0:T(8,128)S(1)} %get-tuple-element.17, f32[2048]{0:T(1024)S(1)} %get-tuple-element.16, f32[2048]{0:T(1024)S(1)} %get-tuple-element.15), kind=kOutput, calls=%fused_computation.32 | convolution fusion | flops 2152726528 | bytes 13647872 | tf_op jit(solution)/shard_map/dot_general | solution.py:36
  71.2 0.0 collective-permute-start
  71.2 2.1 multiply_reduce_fusion.2
  73.3 7.2 %fusion.34 = f32[1024,2048]{1,0:T(8,128)} fusion(bf16[1024,512]{1,0:T(8,128)(2,1)S(1)} %copy-done.2, bf16[2048,512]{1,0:T(8,128)(2,1)} %collective-permute-done.2), kind=kOutput, calls=%fused_computation.50 | convolution fusion | flops 2147483648 | bytes 11534336 | tf_op jit(solution)/shard_map/dot_general | solution.py:16
  80.5 0.5 multiply_reduce_fusion.1
  81.0 2.4 fusion.35
  83.4 7.2 %collective-permute-done.8 = bf16[2048,512]{1,0:T(8,128)(2,1)S(1)} collective-permute-done((bf16[2048,512]{1,0:T(8,128)(2,1)S(1)}, bf16[2048,512]{1,0:T(8,128)(2,1)S(1)}, u32[]{:S(2)}, u32[]{:S(2)}) %collective-permute-start.8) | collective-permute-done | bytes 2097184 | tf_op jit(solution)/shard_map/ppermute | solution.py:12
  90.6 0.5 multiply_reduce_fusion
  91.0 9.7 %fusion.30 = (f32[2048]{0:T(1024)S(1)}, f32[2048]{0:T(1024)S(1)}, f32[2048]{0:T(1024)S(1)}, f32[1024,2048]{1,0:T(8,128)S(1)}) fusion(f32[2048]{0:T(1024)S(1)} %multiply_reduce_fusion, f32[1024]{0:T(1024)S(1)} %multiply_reduce_fusion.4, f32[1024]{0:T(1024)S(1)} %bitcast.15, f32[2048]{0:T(1024)S(1)} %multiply_reduce_fusion.2, f32[1024,2048]{1,0:T(8,128)} %fusion.34, ...), kind=kOutput, calls=%fused_computation.48 | convolution fusion | flops 2191517696 | bytes 28368896 | tf_op jit(solution)/shard_map/dot_general | solution.py:16
  100.8 0.1 collective-permute-start.4
  100.9 34.7 %collective-permute-done.4 = f32[2048]{0:T(1024)S(1)} collective-permute-done((f32[2048]{0:T(1024)S(1)}, f32[2048]{0:T(1024)S(1)}, u32[]{:S(2)}, u32[]{:S(2)}) %collective-permute-start.4) | collective-permute-done | bytes 8224 | tf_op jit(solution)/shard_map/ppermute | solution.py:12
  135.6 1.6 collective-permute-start.10
  137.2 1.5 collective-permute-done.7
  138.7 10.7 %fusion.2 = (f32[2048]{0:T(1024)S(1)}, f32[2048]{0:T(1024)S(1)}, f32[2048]{0:T(1024)S(1)}) fusion(f32[2048]{0:T(1024)S(1)} %max.9, f32[2048]{0:T(1024)S(1)} %multiply_reduce_fusion.2, f32[1024,2048]{1,0:T(8,128)} %fusion.34, f32[1024]{0:T(1024)S(1)} %multiply_reduce_fusion.4, f32[1024]{0:T(1024)S(1)} %bitcast.16, f32[2048]{0:T(1024)S(1)} %max.11, ...), kind=kLoop, calls=%fused_computation.11 | loop fusion | flops 50325504 | bytes 25247744 | tf_op jit(solution)/shard_map/reduce_sum | solution.py:34
  149.5 8.7 %multiply_add_fusion.2 = f32[2048,512]{1,0:T(8,128)S(1)} fusion(f32[2048,512]{1,0:T(8,128)} %collective-permute-done, f32[2048]{0:T(1024)S(1)} %get-tuple-element.13, bf16[1024,512]{1,0:T(8,128)(2,1)S(1)} %copy-done.2, f32[2048]{0:T(1024)S(1)} %max.9, f32[2048]{0:T(1024)S(1)} %multiply_reduce_fusion.2, f32[1024,2048]{1,0:T(8,128)} %fusion.34, ...), kind=kOutput, calls=%fused_computation.28 | convolution fusion | flops 2166358016 | bytes 17858560 | tf_op jit(solution)/shard_map/dot_general | solution.py:36
  158.2 0.1 collective-permute-start.3
  158.3 1.5 collective-permute-start.11
  159.8 46.5 %collective-permute-done.11 = f32[2048]{0:T(1024)S(1)} collective-permute-done((f32[2048]{0:T(1024)S(1)}, f32[2048]{0:T(1024)S(1)}, u32[]{:S(2)}, u32[]{:S(2)}) %collective-permute-start.11) | collective-permute-done | bytes 8224 | tf_op jit(solution)/shard_map/ppermute | solution.py:12
  206.3 4.2 %multiply_add_fusion.1 = f32[2048,512]{1,0:T(8,128)S(1)} fusion(f32[2048,512]{1,0:T(8,128)S(1)} %collective-permute-done.3, f32[2048]{0:T(1024)S(1)} %get-tuple-element.11, bf16[1024,512]{1,0:T(8,128)(2,1)S(1)} %copy-done.2, f32[2048]{0:T(1024)S(1)} %max.10, f32[2048]{0:T(1024)S(1)} %multiply_reduce_fusion.1, f32[1024,2048]{1,0:T(8,128)S(1)} %fusion.35, ...), kind=kOutput, calls=%fused_computation.25 | convolution fusion | flops 2166358016 | bytes 17858560 | tf_op jit(solution)/shard_map/dot_general | solution.py:36
  210.5 0.1 collective-permute-start.6
  210.5 1.5 collective-permute-start.12
  212.1 46.5 %collective-permute-done.12 = f32[2048]{0:T(1024)S(1)} collective-permute-done((f32[2048]{0:T(1024)S(1)}, f32[2048]{0:T(1024)S(1)}, u32[]{:S(2)}, u32[]{:S(2)}) %collective-permute-start.12) | collective-permute-done | bytes 8224 | tf_op jit(solution)/shard_map/ppermute | solution.py:12
  258.6 0.0 copy-start.3
  258.6 0.0 copy-start.1
  258.6 4.2 %multiply_add_fusion = f32[2048,512]{1,0:T(8,128)S(1)} fusion(f32[2048,512]{1,0:T(8,128)S(1)} %collective-permute-done.6, f32[2048]{0:T(1024)S(1)} %get-tuple-element.9, bf16[1024,512]{1,0:T(8,128)(2,1)S(1)} %copy-done.2, f32[2048]{0:T(1024)S(1)} %max.11, f32[2048]{0:T(1024)S(1)} %multiply_reduce_fusion, f32[1024,2048]{1,0:T(8,128)S(1)} %get-tuple-element.18, ...), kind=kOutput, calls=%fused_computation.22 | convolution fusion | flops 2166358016 | bytes 17858560 | tf_op jit(solution)/shard_map/dot_general | solution.py:36
  262.8 0.1 collective-permute-start.9
  262.8 1.5 collective-permute-start.14
  264.4 0.1 collective-permute-start.13
  264.4 46.4 %collective-permute-done.14 = f32[2048]{0:T(1024)S(1)} collective-permute-done((f32[2048]{0:T(1024)S(1)}, f32[2048]{0:T(1024)S(1)}, u32[]{:S(2)}, u32[]{:S(2)}) %collective-permute-start.14) | collective-permute-done | bytes 8224 | tf_op jit(solution)/shard_map/ppermute | solution.py:12
  310.8 0.1 collective-permute-done.13
  310.9 0.6 subtract_multiply_fusion.4
  311.5 2.4 broadcast_divide_fusion
  (22 shorter events, 0.1 us)
Async XLA Ops:
  7.2 1.6 copy-start
  7.2 50.3 %all-gather.4.cloned.1.call-start = ((), (), s32[]{:S(2)}) async-start(), calls=%async_computation | async-start | bytes 1179648 | tf_op jit(solution)/shard_map/all_gather | solution.py:52
  7.2 26.5 %collective-permute-start.2 = (bf16[2048,512]{1,0:T(8,128)(2,1)}, bf16[2048,512]{1,0:T(8,128)(2,1)}, u32[]{:S(2)}, u32[]{:S(2)}) collective-permute-start(bf16[2048,512]{1,0:T(8,128)(2,1)} %param.8), channel_id=1, source_target_pairs={{24,0},{0,8},{8,16},{16,24},{25,1},{1,9},{9,17},{17,25},{26,2},{2,... | collective-permute-start | bytes 6291464 | tf_op jit(solution)/shard_map/ppermute | solution.py:12
  33.7 31.4 %collective-permute-start.5 = (bf16[2048,512]{1,0:T(8,128)(2,1)}, bf16[2048,512]{1,0:T(8,128)(2,1)S(1)}, u32[]{:S(2)}, u32[]{:S(2)}) collective-permute-start(bf16[2048,512]{1,0:T(8,128)(2,1)} %collective-permute-done.2), channel_id=1, source_target_pairs={{24,0},{0,8},{8,16},{16,24},{25,1},{1,9},{9,17},{17,25},{26,2},{2,... | collective-permute-start | bytes 6291464 | tf_op jit(solution)/shard_map/ppermute | solution.py:12
  63.8 2.9 copy-start.2
  63.8 37.0 %collective-permute-start.1 = (f32[2048]{0:T(1024)S(1)}, f32[2048]{0:T(1024)S(1)}, u32[]{:S(2)}, u32[]{:S(2)}) collective-permute-start(f32[2048]{0:T(1024)S(1)} %get-tuple-element.16), channel_id=1, source_target_pairs={{24,0},{0,8},{8,16},{16,24},{25,1},{1,9},{9,17},{17,25},{26,2},{2,... | collective-permute-start | bytes 24584 | tf_op jit(solution)/shard_map/ppermute | solution.py:12
  65.1 25.5 %collective-permute-start.8 = (bf16[2048,512]{1,0:T(8,128)(2,1)S(1)}, bf16[2048,512]{1,0:T(8,128)(2,1)S(1)}, u32[]{:S(2)}, u32[]{:S(2)}) collective-permute-start(bf16[2048,512]{1,0:T(8,128)(2,1)S(1)} %collective-permute-done.5), channel_id=1, source_target_pairs={{24,0},{0,8},{8,16},{16,24},{25,1},{1,9},{9,17},{17,25},{26,2},{2,... | collective-permute-start | bytes 6291464 | tf_op jit(solution)/shard_map/ppermute | solution.py:12
  71.2 78.3 %collective-permute-start = (f32[2048,512]{1,0:T(8,128)}, f32[2048,512]{1,0:T(8,128)}, u32[]{:S(2)}, u32[]{:S(2)}) collective-permute-start(f32[2048,512]{1,0:T(8,128)} %fusion.20), channel_id=1, source_target_pairs={{24,0},{0,8},{8,16},{16,24},{25,1},{1,9},{9,17},{17,25},{26,2},{2,... | collective-permute-start | bytes 12582920 | tf_op jit(solution)/shard_map/ppermute | solution.py:12
  100.8 34.8 %collective-permute-start.4 = (f32[2048]{0:T(1024)S(1)}, f32[2048]{0:T(1024)S(1)}, u32[]{:S(2)}, u32[]{:S(2)}) collective-permute-start(f32[2048]{0:T(1024)S(1)} %max.9), channel_id=1, source_target_pairs={{24,0},{0,8},{8,16},{16,24},{25,1},{1,9},{9,17},{17,25},{26,2},{2,... | collective-permute-start | bytes 24584 | tf_op jit(solution)/shard_map/ppermute | solution.py:12
  135.6 3.1 collective-permute-start.7
  135.6 13.8 %collective-permute-start.10 = (f32[2048]{0:T(1024)S(1)}, f32[2048]{0:T(1024)S(1)}, u32[]{:S(2)}, u32[]{:S(2)}) collective-permute-start(f32[2048]{0:T(1024)S(1)} %get-tuple-element.14), channel_id=1, source_target_pairs={{24,0},{0,8},{8,16},{16,24},{25,1},{1,9},{9,17},{17,25},{26,2},{2,... | collective-permute-start | bytes 24584 | tf_op jit(solution)/shard_map/ppermute | solution.py:12
  158.2 48.1 %collective-permute-start.3 = (f32[2048,512]{1,0:T(8,128)S(1)}, f32[2048,512]{1,0:T(8,128)S(1)}, u32[]{:S(2)}, u32[]{:S(2)}) collective-permute-start(f32[2048,512]{1,0:T(8,128)S(1)} %multiply_add_fusion.2), channel_id=1, source_target_pairs={{24,0},{0,8},{8,16},{16,24},{25,1},{1,9},{9,17},{17,25},{26,2},{2,... | collective-permute-start | bytes 12582920 | tf_op jit(solution)/shard_map/ppermute | solution.py:12
  158.3 48.0 %collective-permute-start.11 = (f32[2048]{0:T(1024)S(1)}, f32[2048]{0:T(1024)S(1)}, u32[]{:S(2)}, u32[]{:S(2)}) collective-permute-start(f32[2048]{0:T(1024)S(1)} %get-tuple-element.12), channel_id=1, source_target_pairs={{24,0},{0,8},{8,16},{16,24},{25,1},{1,9},{9,17},{17,25},{26,2},{2,... | collective-permute-start | bytes 24584 | tf_op jit(solution)/shard_map/ppermute | solution.py:12
  210.5 48.1 %collective-permute-start.6 = (f32[2048,512]{1,0:T(8,128)S(1)}, f32[2048,512]{1,0:T(8,128)S(1)}, u32[]{:S(2)}, u32[]{:S(2)}) collective-permute-start(f32[2048,512]{1,0:T(8,128)S(1)} %multiply_add_fusion.1), channel_id=1, source_target_pairs={{24,0},{0,8},{8,16},{16,24},{25,1},{1,9},{9,17},{17,25},{26,2},{2,... | collective-permute-start | bytes 12582920 | tf_op jit(solution)/shard_map/ppermute | solution.py:12
  210.5 48.0 %collective-permute-start.12 = (f32[2048]{0:T(1024)S(1)}, f32[2048]{0:T(1024)S(1)}, u32[]{:S(2)}, u32[]{:S(2)}) collective-permute-start(f32[2048]{0:T(1024)S(1)} %get-tuple-element.10), channel_id=1, source_target_pairs={{24,0},{0,8},{8,16},{16,24},{25,1},{1,9},{9,17},{17,25},{26,2},{2,... | collective-permute-start | bytes 24584 | tf_op jit(solution)/shard_map/ppermute | solution.py:12
  258.6 52.4 %copy-start.3 = (f32[2048]{0:T(1024)S(1)}, f32[2048]{0:T(1024)}, u32[]{:S(2)}) copy-start(f32[2048]{0:T(1024)} %param.9) | copy-start | bytes 24580
  258.6 55.3 %copy-start.1 = (bf16[2048,512]{1,0:T(8,128)(2,1)S(1)}, bf16[2048,512]{1,0:T(8,128)(2,1)}, u32[]{:S(2)}) copy-start(bf16[2048,512]{1,0:T(8,128)(2,1)} %param.5) | copy-start | bytes 6291460
  262.8 48.8 %collective-permute-start.9 = (f32[2048,512]{1,0:T(8,128)S(1)}, f32[2048,512]{1,0:T(8,128)S(1)}, u32[]{:S(2)}, u32[]{:S(2)}) collective-permute-start(f32[2048,512]{1,0:T(8,128)S(1)} %multiply_add_fusion), channel_id=1, source_target_pairs={{24,0},{0,8},{8,16},{16,24},{25,1},{1,9},{9,17},{17,25},{26,2},{2,... | collective-permute-start | bytes 12582920 | tf_op jit(solution)/shard_map/ppermute | solution.py:12
  262.8 48.0 %collective-permute-start.14 = (f32[2048]{0:T(1024)S(1)}, f32[2048]{0:T(1024)S(1)}, u32[]{:S(2)}, u32[]{:S(2)}) collective-permute-start(f32[2048]{0:T(1024)S(1)} %max.11), channel_id=1, source_target_pairs={{24,0},{0,8},{8,16},{16,24},{25,1},{1,9},{9,17},{17,25},{26,2},{2,... | collective-permute-start | bytes 24584 | tf_op jit(solution)/shard_map/ppermute | solution.py:12
  264.4 46.5 %collective-permute-start.13 = (f32[2048]{0:T(1024)S(1)}, f32[2048]{0:T(1024)S(1)}, u32[]{:S(2)}, u32[]{:S(2)}) collective-permute-start(f32[2048]{0:T(1024)S(1)} %get-tuple-element.8), channel_id=1, source_target_pairs={{24,0},{0,8},{8,16},{16,24},{25,1},{1,9},{9,17},{17,25},{26,2},{2,... | collective-permute-start | bytes 24584 | tf_op jit(solution)/shard_map/ppermute | solution.py:12
Sparse Core Ops, SparseCore 0:
  10.7 42.7 all-gather.3
where the time goes:
time: 321 us
  waiting for transfers between devices  206 us (64%)
  matrix products  45.6 us (14%)
  other arithmetic  22.3 us (7%)
  blocking collectives  21.7 us (7%)
  between operations  14.3 us (4%)
  starting transfers between devices  8.72 us (3%)
    ppermute x15, waiting for transfers between devices, shifted(): return lax.ppermute(block, axis, route)  206 us
    dot_general x4, matrix products, column_scores(): lax.dot_general(rows, panel, (((1,), (1,)), ((), ())), preferred_element_...  24 us
    all_gather x1, blocking collectives, group_gather(): lax.all_gather(potentials, 'grp', axis=0, tiled=True)  21.7 us
    dot_general x4, matrix products, visit(): lax.dot_general(weights, rows, (((0,), (0,)), ((), ())), preferred_elemen...  21.6 us
    reduce_sum x2, other arithmetic, visit(): mass = mass * shrink + jnp.sum(expd, axis=0)  11.9 us
    ppermute x15, starting transfers between devices, shifted(): return lax.ppermute(block, axis, route)  8.69 us
  transfers between devices with their start and end apart: 16, of which 8 were waited for; matrix products, arithmetic and copies ran while one was open for 16% of the time, Pallas kernels for 0%

commit v1 on v0

v1 whole, which is shorter than its diff:
```python
import functools
import math

import jax
import jax.numpy as jnp
from jax import lax
from jax.experimental import pallas as pl
from jax.experimental.pallas import tpu as pltpu
from jax.sharding import PartitionSpec as P

BF16, F32 = jnp.bfloat16, jnp.float32
AXES = ("blk", "grp")
EXTRA = 16
LANES = 128
VMEM = pl.BlockSpec(memory_space=pltpu.VMEM)
NT = (((1,), (1,)), ((), ()))


def in_vmem(array):
    return pltpu.with_memory_space_constraint(array, pltpu.VMEM)


def eye():
    shape = (LANES, LANES)
    return lax.broadcasted_iota(jnp.int32, shape, 0) == lax.broadcasted_iota(jnp.int32, shape, 1)


def to_row(column):
    return jnp.sum(jnp.where(eye(), column, 0.0), axis=0, keepdims=True)


def to_column(row):
    return jnp.sum(jnp.where(eye(), row, 0.0), axis=1, keepdims=True)


def gather_kernel(table_ref, ids_ref, pots_ref, out_ref):
    records, width = table_ref.shape
    count = ids_ref.shape[1]
    step = 512
    column = to_column(ids_ref[...].astype(F32)).astype(jnp.int32)
    rows = jnp.zeros((count, width), F32)
    for first in range(0, records, step):
        spot = lax.broadcasted_iota(jnp.int32, (count, step), 1) + first
        pick = jnp.where(spot == column, 1.0, 0.0).astype(BF16)
        rows += jnp.dot(pick, table_ref[first : first + step, :], preferred_element_type=F32)
    norm = to_row(jnp.sum(jnp.square(rows), axis=1, keepdims=True))
    term = pots_ref[...].astype(F32) * (width / 2) - 0.5 * norm
    high = term.astype(BF16).astype(F32)
    middle = (term - high).astype(BF16).astype(F32)
    low = term - high - middle
    line = lax.broadcasted_iota(jnp.int32, (EXTRA, LANES), 0)
    parts = jnp.where(line == 0, high, jnp.where(line == 1, middle, jnp.where(line == 2, low, 0.0)))
    out_ref[0:count, :] = rows.astype(BF16)
    out_ref[count:, :] = jnp.zeros((EXTRA, width), BF16)
    out_ref[count:, 0:LANES] = parts.astype(BF16)


def gather(table, row_ids, potentials):
    count, width = row_ids.shape[0], table.shape[1]
    return pl.pallas_call(
        gather_kernel,
        out_shape=pltpu.VMEM((count + EXTRA, width), BF16),
        in_specs=[VMEM] * 3,
        out_specs=VMEM,
        compiler_params=pltpu.CompilerParams(vmem_limit_bytes=16 << 20),
        name="gather",
    )(table, row_ids.reshape(1, count), potentials.reshape(1, count))


def pieces(refs, count):
    rows, terms = [], []
    for ref in refs:
        for first in range(0, ref.shape[0], count + EXTRA):
            rows.append(ref[first : first + count, :])
            extra = ref[first + count : first + count + EXTRA, 0:LANES].astype(F32)
            terms.append(jnp.sum(extra, axis=0, keepdims=True))
    return rows, terms


def block_step(centres, rows, terms, alpha, old):
    shifted = lax.dot_general(centres, rows, NT, preferred_element_type=F32) + terms
    top = jnp.max(shifted, axis=1, keepdims=True)
    if old is not None:
        top = jnp.maximum(old[0], top)
    expd = jnp.exp2((shifted - top) * alpha)
    mass = expd[:, 0:LANES]
    for first in range(LANES, expd.shape[1], LANES):
        mass = mass + expd[:, first : first + LANES]
    numer = jnp.dot(expd.astype(BF16), rows, preferred_element_type=F32)
    if old is not None:
        shrink = jnp.exp2((old[0] - top) * alpha)
        mass = old[1] * shrink + mass
        numer = old[2] * shrink + numer
    return top, mass, numer


def visit_kernel(shards, count, block, chunk, first, last, scale, *refs):
    shard_refs, refs = refs[:shards], refs[shards:]
    centres_ref, refs = refs[0], refs[1:]
    state_in, refs = (None, refs) if first else (refs[:3], refs[3:])
    balance_ref, refs = (refs[0], refs[1:]) if last else (None, refs)
    width = centres_ref.shape[1]
    alpha = math.log2(math.e) * 2.0 * scale / width
    rows, terms = pieces(shard_refs, count)
    per = max(1, chunk // count)
    groups = [
        (jnp.concatenate(rows[i : i + per], axis=0), jnp.concatenate(terms[i : i + per], axis=1))
        for i in range(0, len(rows), per)
    ]

    def one(j, _):
        at = pl.ds(pl.multiple_of(j * block, block), block)
        centres = centres_ref[at, :]
        state = None if first else (state_in[0][at, 0:1], state_in[1][at, :], state_in[2][at, :])
        for group_rows, group_terms in groups:
            state = block_step(centres, group_rows, group_terms, alpha, state)
        top, mass, numer = state
        if not last:
            refs[0][at, :] = jnp.broadcast_to(top, (block, LANES))
            refs[1][at, :] = mass
            refs[2][at, :] = numer
            return 0
        means_ref, potential_ref = refs
        mass = jnp.sum(mass, axis=1, keepdims=True)
        means_ref[at, :] = numer / mass
        centre = jnp.sum(jnp.square(centres.astype(F32)), axis=1, keepdims=True)
        peak = (scale / width) * (2.0 * top - centre)
        for i in range(block // LANES):
            part = slice(i * LANES, (i + 1) * LANES)
            line = pl.ds(j * (block // LANES) + i, 1)
            potential_ref[line, :] = (
                jnp.log(balance_ref[line, :]) - to_row(peak[part]) - jnp.log(to_row(mass[part]))
            ) / scale
        return 0

    lax.fori_loop(0, centres_ref.shape[0] // block, one, 0)


def visit(shards, count, centroids, state, scale, balance=None, chunk=512):
    total, width = centroids.shape
    block = min(1024, total)
    first, last = state is None, balance is not None
    number = sum(s.shape[0] // (count + EXTRA) for s in shards)
    if last:
        out_shape = (
            jax.ShapeDtypeStruct((total, width), F32),
            jax.ShapeDtypeStruct((total // LANES, LANES), F32),
        )
    else:
        out_shape = (
            pltpu.VMEM((total, LANES), F32),
            pltpu.VMEM((total, LANES), F32),
            pltpu.VMEM((total, width), F32),
        )
    args = [in_vmem(s) for s in shards] + [in_vmem(centroids)]
    aliases = {}
    if not first:
        if not last:
            aliases = {len(args) + i: i for i in range(3)}
        args += [in_vmem(s) for s in state]
    if last:
        args.append(balance.reshape(total // LANES, LANES))
    rows = number * count
    return pl.pallas_call(
        functools.partial(visit_kernel, len(shards), count, block, chunk, first, last, scale),
        out_shape=out_shape,
        in_specs=[VMEM] * len(args),
        out_specs=tuple([VMEM] * len(out_shape)),
        input_output_aliases=aliases,
        compiler_params=pltpu.CompilerParams(vmem_limit_bytes=40 << 20),
        cost_estimate=pl.CostEstimate(
            flops=4 * rows * total * width, bytes_accessed=4 * total * width, transcendentals=rows * total
        ),
        name="visit",
    )(*args)


def pack(parts):
    return parts[0] if len(parts) == 1 else jnp.concatenate(parts, axis=0)


def body(table, row_ids, potentials, centroids, balance):
    scale = 1.5 * math.sqrt(table.shape[1])
    count = row_ids.shape[0]
    blk, grp = lax.axis_size("blk"), lax.axis_size("grp")

    def swap(array, flip):
        route = [(i, flip(i // grp, i % grp)) for i in range(blk * grp)]
        return lax.ppermute(array, AXES, route)

    def core(array):
        return swap(array, lambda b, g: (b ^ 1) * grp + g)

    def grp_bit(array, bit):
        return swap(array, lambda b, g: b * grp + (g ^ bit))

    def one_way(array):
        return swap(array, lambda b, g: b * grp + (g ^ 1) if b & 1 else (b ^ 2) * grp + g)

    def other_way(array):
        return swap(array, lambda b, g: (b ^ 2) * grp + g if b & 1 else b * grp + (g ^ 1))

    own = gather(table, row_ids, potentials)
    bit = grp // 2
    while bit > 4:
        own = pack([own, grp_bit(own, bit)])
        bit //= 2
    near = grp_bit(own, 2)
    far = grp_bit(own, 4)
    state = visit([own, core(own)], count, centroids, None, scale)
    pair = pack([own, near])
    x_pair = one_way(pair)
    state = visit([near, core(near)], count, centroids, state, scale)
    y_pair = other_way(pair)
    both = grp_bit(far, 2)
    state = visit([far, core(far)], count, centroids, state, scale)
    xy_pair = other_way(x_pair)
    state = visit([x_pair, core(x_pair)], count, centroids, state, scale)
    late = pack([far, both])
    x_late = one_way(late)
    y_late = other_way(late)
    state = visit([y_pair, core(y_pair), both, core(both)], count, centroids, state, scale)
    xy_late = other_way(x_late)
    state = visit([xy_pair, core(xy_pair)], count, centroids, state, scale)
    state = visit([x_late, core(x_late), y_late, core(y_late)], count, centroids, state, scale)
    means, potential = visit([xy_late, core(xy_late)], count, centroids, state, scale, balance)
    return means, potential.reshape(balance.shape)


def solution(mesh):
    placed = (
        P(AXES, None),
        P(AXES),
        P(AXES),
        P(AXES, None),
        P(AXES),
    )
    return jax.shard_map(
        body,
        mesh=mesh,
        in_specs=placed,
        out_specs=(P(AXES, None), P(AXES)),
        check_vma=False,
    )
```

time: 321 us -> 79.3 us (0.25)
  waiting for transfers between devices: 206 us -> 7.92 us
  Pallas kernels: 0 us -> 49 us
  matrix products: 45.6 us -> 0 us
  other arithmetic: 22.3 us -> 0.02 us
  blocking collectives: 21.7 us -> 0 us
  between operations: 14.3 us -> 0.81 us
  starting transfers between devices: 8.72 us -> 16.6 us
    ppermute x15 -> x19, waiting for transfers between devices: 206 us -> 7.92 us  [swap(): return lax.ppermute(array, AXES, route)]
    pallas_call x0 -> x9, Pallas kernels: none -> 49 us  [the longest x8 48.4 us: visit(): pl.pallas_call(functools.partial(visit_kernel, len(shards), count, block,...]
    dot_general x8 -> x0, matrix products: 45.6 us -> none  [the longest x4 24 us: column_scores(): lax.dot_general(rows, panel, (((1,), (1,)), ((), ())), preferred_element_...]
    all_gather x1 -> x0, blocking collectives: 21.7 us -> none  [group_gather(): lax.all_gather(potentials, 'grp', axis=0, tiled=True)]
    reduce_sum x7 -> x0, other arithmetic: 18.5 us -> none  [the longest x2 11.9 us: visit(): mass = mass * shrink + jnp.sum(expd, axis=0)]
    ppermute x15 -> x19, starting transfers between devices: 8.69 us -> 16.6 us  [swap(): return lax.ppermute(array, AXES, route)]
    unnamed x8 -> x13, local copies, waits for them, and re-layouts: 0.32 us -> 4.66 us
  transfers between devices with their start and end apart: 16 -> 19, of which waited for: 8 -> 3; matrix products, arithmetic and copies ran while one was open for 16% -> 0% of each run, Pallas kernels for 0% -> 51%
where the time goes in v1:
time: 79.3 us; the launch traced here: 79.1 us
  Pallas kernels  49 us (62%)
  starting transfers between devices  16.6 us (21%)
  waiting for transfers between devices  7.92 us (10%)
  local copies, waits for them, and re-layouts  4.67 us (6%)
  between operations  0.81 us (1%)
    pallas_call x8, Pallas kernels, visit(): pl.pallas_call(functools.partial(visit_kernel, len(shards), count, block,...  48.4 us
    ppermute x19, starting transfers between devices, swap(): return lax.ppermute(array, AXES, route)  16.6 us
    ppermute x19, waiting for transfers between devices, swap(): return lax.ppermute(array, AXES, route)  7.92 us
    unnamed x13, local copies, waits for them, and re-layouts  4.66 us
  transfers between devices with their start and end apart: 19, of which 3 were waited for; matrix products, arithmetic and copies ran while one was open for 0% of the time, Pallas kernels for 51%

profile of v1, /device:TPU:0, one launch (start us, length us, event | category | flops | bytes accessed | tf_op | source)
XLA Modules:
  0.0 79.1 jit_solution(6465755151446151353)
XLA Ops:
  0.6 0.0 copy-start.1
  0.7 1.7 %copy-done.2 = bf16[2048,512]{1,0:T(8,128)(2,1)S(1)} copy-done((bf16[2048,512]{1,0:T(8,128)(2,1)S(1)}, bf16[2048,512]{1,0:T(8,128)(2,1)}, u32[]{:S(2)}) %copy-start.2) | copy-done | bytes 2097176
  2.4 0.7 copy-done.4
  3.0 0.7 copy-done.5
  3.7 0.6 gather.1.refs_0_
  4.3 3.1 %collective-permute-start.8 = (bf16[144,512]{1,0:T(8,128)(2,1)S(1)}, bf16[144,512]{1,0:T(8,128)(2,1)S(1)}, u32[]{:S(2)}, u32[]{:S(2)}) collective-permute-start(bf16[144,512]{1,0:T(8,128)(2,1)S(1)} %gather.1.refs_0_), channel_id=1, source_target_pairs={{0,2},{1,3},{2,0},{3,1},{4,6},{5,7},{6,4},{7,5},{8,10},{9,11},{10,... | collective-permute-start | bytes 442376 | tf_op jit(solution)/shard_map/ppermute | solution.py:189
  7.4 2.6 %collective-permute-start = (bf16[144,512]{1,0:T(8,128)(2,1)S(1)}, bf16[144,512]{1,0:T(8,128)(2,1)S(1)}, u32[]{:S(2)}, u32[]{:S(2)}) collective-permute-start(bf16[144,512]{1,0:T(8,128)(2,1)S(1)} %gather.1.refs_0_), channel_id=1, source_target_pairs={{0,4},{1,5},{2,6},{3,7},{4,0},{5,1},{6,2},{7,3},{8,12},{9,13},{10,... | collective-permute-start | bytes 442376 | tf_op jit(solution)/shard_map/ppermute | solution.py:189
  10.0 3.8 %collective-permute-done.8.refs_0_ = bf16[144,512]{1,0:T(8,128)(2,1)S(1)} collective-permute-done((bf16[144,512]{1,0:T(8,128)(2,1)S(1)}, bf16[144,512]{1,0:T(8,128)(2,1)S(1)}, u32[]{:S(2)}, u32[]{:S(2)}) %collective-permute-start.8) | collective-permute-done | bytes 147488 | tf_op jit(solution)/shard_map/ppermute | solution.py:189
  13.8 1.9 %collective-permute-start.9 = (bf16[288,512]{1,0:T(8,128)(2,1)S(1)}, bf16[288,512]{1,0:T(8,128)(2,1)S(1)}, u32[]{:S(2)}, u32[]{:S(2)}) collective-permute-start(bf16[288,512]{1,0:T(8,128)(2,1)S(1)} %pad_maximum_fusion), channel_id=1, source_target_pairs={{0,16},{1,17},{2,18},{3,19},{4,20},{5,21},{6,22},{7,23},{8,9},{9,8... | collective-permute-start | bytes 884744 | tf_op jit(solution)/shard_map/ppermute | solution.py:189
  15.7 1.1 %collective-permute-done.refs_0_ = bf16[144,512]{1,0:T(8,128)(2,1)S(1)} collective-permute-done((bf16[144,512]{1,0:T(8,128)(2,1)S(1)}, bf16[144,512]{1,0:T(8,128)(2,1)S(1)}, u32[]{:S(2)}, u32[]{:S(2)}) %collective-permute-start) | collective-permute-done | bytes 147488 | tf_op jit(solution)/shard_map/ppermute | solution.py:189
  16.8 0.4 collective-permute-start.1
  17.2 0.0 collective-permute-start.18
  17.2 1.5 %collective-permute-start.12 = (bf16[288,512]{1,0:T(8,128)(2,1)S(1)}, bf16[288,512]{1,0:T(8,128)(2,1)S(1)}, u32[]{:S(2)}, u32[]{:S(2)}) collective-permute-start(bf16[288,512]{1,0:T(8,128)(2,1)S(1)} %pad_maximum_fusion), channel_id=1, source_target_pairs={{0,1},{1,0},{2,3},{3,2},{4,5},{5,4},{6,7},{7,6},{8,24},{9,25},{10,... | collective-permute-start | bytes 884744 | tf_op jit(solution)/shard_map/ppermute | solution.py:189
  18.8 0.2 collective-permute-start.17
  19.0 3.0 %collective-permute-done.1.refs_2_ = bf16[144,512]{1,0:T(8,128)(2,1)S(1)} collective-permute-done((bf16[144,512]{1,0:T(8,128)(2,1)S(1)}, bf16[144,512]{1,0:T(8,128)(2,1)S(1)}, u32[]{:S(2)}, u32[]{:S(2)}) %collective-permute-start.1) | collective-permute-done | bytes 147488 | tf_op jit(solution)/shard_map/ppermute | solution.py:189
  21.9 0.0 collective-permute-start.16
  22.0 0.0 collective-permute-done.18.refs_1_
  22.0 1.6 %collective-permute-start.2 = (bf16[288,512]{1,0:T(8,128)(2,1)S(1)}, bf16[288,512]{1,0:T(8,128)(2,1)S(1)}, u32[]{:S(2)}, u32[]{:S(2)}) collective-permute-start(bf16[288,512]{1,0:T(8,128)(2,1)S(1)} %constant_dynamic-update-slice_fusion), channel_id=1, source_target_pairs={{0,16},{1,17},{2,18},{3,19},{4,20},{5,21},{6,22},{7,23},{8,9},{9,8... | collective-permute-start | bytes 884744 | tf_op jit(solution)/shard_map/ppermute | solution.py:189
  23.5 0.0 collective-permute-done.9.refs_0_
  23.5 0.3 collective-permute-start.15
  23.8 1.6 %copy-done = bf16[2048,512]{1,0:T(8,128)(2,1)S(1)} copy-done((bf16[2048,512]{1,0:T(8,128)(2,1)S(1)}, bf16[2048,512]{1,0:T(8,128)(2,1)}, u32[]{:S(2)}) %copy-start) | copy-done | bytes 2097176
  25.4 2.4 %visit.8 = (f32[2048,128]{1,0:T(8,128)S(1)}, f32[2048,128]{1,0:T(8,128)S(1)}, f32[2048,512]{1,0:T(8,128)S(1)}) custom-call(bf16[144,512]{1,0:T(8,128)(2,1)S(1)} %gather.1.refs_0_, bf16[144,512]{1,0:T(8,128)(2,1)S(1)} %collective-permute-done.18.refs_1_, bf16[2048,512]{1,0:T(8,128)(2,1)S(1)} %copy-done), custom_call_target="tpu_custom_call" | custom-call | flops 1073741824 | bytes 4194304 | tf_op jit(solution)/shard_map/visit/pallas_call | solution.py:164
  27.8 0.0 collective-permute-done.17.refs_1_
  27.8 1.3 %collective-permute-start.6 = (bf16[288,512]{1,0:T(8,128)(2,1)S(1)}, bf16[288,512]{1,0:T(8,128)(2,1)S(1)}, u32[]{:S(2)}, u32[]{:S(2)}) collective-permute-start(bf16[288,512]{1,0:T(8,128)(2,1)S(1)} %constant_dynamic-update-slice_fusion), channel_id=1, source_target_pairs={{0,1},{1,0},{2,3},{3,2},{4,5},{5,4},{6,7},{7,6},{8,24},{9,25},{10,... | collective-permute-start | bytes 884744 | tf_op jit(solution)/shard_map/ppermute | solution.py:189
  29.2 4.8 %visit.9 = (f32[2048,128]{1,0:T(8,128)S(1)}, f32[2048,128]{1,0:T(8,128)S(1)}, f32[2048,512]{1,0:T(8,128)S(1)}) custom-call(bf16[144,512]{1,0:T(8,128)(2,1)S(1)} %collective-permute-done.8.refs_0_, bf16[144,512]{1,0:T(8,128)(2,1)S(1)} %collective-permute-done.17.refs_1_, ...), custom_call_target="tpu_custom_call", output_to_operand_aliasing={{0}: (3, {}), {1}: (4, {}), {2}: (5, {})} | custom-call | flops 1073741824 | bytes 4194304 | tf_op jit(solution)/shard_map/visit/pallas_call | solution.py:164
  33.9 0.0 collective-permute-done.16.refs_1_
  33.9 0.8 %collective-permute-start.10 = (bf16[288,512]{1,0:T(8,128)(2,1)S(1)}, bf16[288,512]{1,0:T(8,128)(2,1)S(1)}, u32[]{:S(2)}, u32[]{:S(2)}) collective-permute-start(bf16[288,512]{1,0:T(8,128)(2,1)S(1)} %collective-permute-done.9.refs_0_), channel_id=1, source_target_pairs={{0,1},{1,0},{2,3},{3,2},{4,5},{5,4},{6,7},{7,6},{8,24},{9,25},{10,... | collective-permute-start | bytes 884744 | tf_op jit(solution)/shard_map/ppermute | solution.py:189
  34.8 4.8 %visit.10 = (f32[2048,128]{1,0:T(8,128)S(1)}, f32[2048,128]{1,0:T(8,128)S(1)}, f32[2048,512]{1,0:T(8,128)S(1)}) custom-call(bf16[144,512]{1,0:T(8,128)(2,1)S(1)} %collective-permute-done.refs_0_, bf16[144,512]{1,0:T(8,128)(2,1)S(1)} %collective-permute-done.16.refs_1_, ...), custom_call_target="tpu_custom_call", output_to_operand_aliasing={{0}: (3, {}), {1}: (4, {}), {2}: (5, {})} | custom-call | flops 1073741824 | bytes 4194304 | tf_op jit(solution)/shard_map/visit/pallas_call | solution.py:164
  39.5 0.6 collective-permute-start.14
  40.1 0.0 collective-permute-done.15.refs_1_
  40.1 0.1 collective-permute-start.5
  40.2 5.2 %visit.11 = (f32[2048,128]{1,0:T(8,128)S(1)}, f32[2048,128]{1,0:T(8,128)S(1)}, f32[2048,512]{1,0:T(8,128)S(1)}) custom-call(bf16[288,512]{1,0:T(8,128)(2,1)S(1)} %collective-permute-done.9.refs_0_, bf16[288,512]{1,0:T(8,128)(2,1)S(1)} %collective-permute-done.15.refs_1_, ...), custom_call_target="tpu_custom_call", output_to_operand_aliasing={{0}: (3, {}), {1}: (4, {}), {2}: (5, {})} | custom-call | flops 2147483648 | bytes 4194304 | tf_op jit(solution)/shard_map/visit/pallas_call | solution.py:164
  45.4 1.3 %collective-permute-start.3 = (bf16[288,512]{1,0:T(8,128)(2,1)S(1)}, bf16[288,512]{1,0:T(8,128)(2,1)S(1)}, u32[]{:S(2)}, u32[]{:S(2)}) collective-permute-start(bf16[288,512]{1,0:T(8,128)(2,1)S(1)} %collective-permute-done.2.refs_0_), channel_id=1, source_target_pairs={{0,1},{1,0},{2,3},{3,2},{4,5},{5,4},{6,7},{7,6},{8,24},{9,25},{10,... | collective-permute-start | bytes 884744 | tf_op jit(solution)/shard_map/ppermute | solution.py:189
  46.8 0.0 collective-permute-done.6.refs_2_
  46.8 0.4 collective-permute-start.7
  47.1 0.1 collective-permute-start.11
  47.3 0.0 collective-permute-done.13.refs_1_
  47.3 8.7 %visit.12 = (f32[2048,128]{1,0:T(8,128)S(1)}, f32[2048,128]{1,0:T(8,128)S(1)}, f32[2048,512]{1,0:T(8,128)S(1)}) custom-call(bf16[288,512]{1,0:T(8,128)(2,1)S(1)} %collective-permute-done.12.refs_0_, bf16[288,512]{1,0:T(8,128)(2,1)S(1)} %collective-permute-done.13.refs_1_, ...), custom_call_target="tpu_custom_call", output_to_operand_aliasing={{0}: (5, {}), {1}: (6, {}), {2}: (7, {})} | custom-call | flops 3221225472 | bytes 4194304 | tf_op jit(solution)/shard_map/visit/pallas_call | solution.py:164
  56.0 0.0 collective-permute-done.3.refs_0_
  56.0 0.4 collective-permute-start.4
  56.4 0.0 collective-permute-done.11.refs_1_
  56.4 5.4 %visit.13 = (f32[2048,128]{1,0:T(8,128)S(1)}, f32[2048,128]{1,0:T(8,128)S(1)}, f32[2048,512]{1,0:T(8,128)S(1)}) custom-call(bf16[288,512]{1,0:T(8,128)(2,1)S(1)} %collective-permute-done.10.refs_0_, bf16[288,512]{1,0:T(8,128)(2,1)S(1)} %collective-permute-done.11.refs_1_, ...), custom_call_target="tpu_custom_call", output_to_operand_aliasing={{0}: (3, {}), {1}: (4, {}), {2}: (5, {})} | custom-call | flops 2147483648 | bytes 4194304 | tf_op jit(solution)/shard_map/visit/pallas_call | solution.py:164
  61.8 0.0 collective-permute-done.5.refs_1_
  61.8 0.0 collective-permute-done.7.refs_3_
  61.8 0.0 copy-start.3
  61.8 8.9 %visit.14 = (f32[2048,128]{1,0:T(8,128)S(1)}, f32[2048,128]{1,0:T(8,128)S(1)}, f32[2048,512]{1,0:T(8,128)S(1)}) custom-call(bf16[288,512]{1,0:T(8,128)(2,1)S(1)} %collective-permute-done.2.refs_0_, bf16[288,512]{1,0:T(8,128)(2,1)S(1)} %collective-permute-done.5.refs_1_, ...), custom_call_target="tpu_custom_call", output_to_operand_aliasing={{0}: (5, {}), {1}: (6, {}), {2}: (7, {})} | custom-call | flops 4294967296 | bytes 4194304 | tf_op jit(solution)/shard_map/visit/pallas_call | solution.py:164
  70.7 0.0 collective-permute-done.4.refs_1_
  70.7 8.3 %visit.15 = (f32[2048,512]{1,0:T(8,128)}, f32[16,128]{1,0:T(8,128)}) custom-call(bf16[288,512]{1,0:T(8,128)(2,1)S(1)} %collective-permute-done.3.refs_0_, bf16[288,512]{1,0:T(8,128)(2,1)S(1)} %collective-permute-done.4.refs_1_, bf16[2048,512]{1,0:T(8,128)(2,1)S(1)} %copy-done.1, f32[2048,128]{1,0:T(8,128)S(1)} %get-tuple-element.43.refs_3_, ...), custom_call_target="tpu_custom_call" | custom-call | flops 2147483648 | bytes 4194304 | tf_op jit(solution)/shard_map/visit/pallas_call | solution.py:164
  (14 shorter events, 0.1 us)
Async XLA Ops:
  0.6 28.5 %copy-start.1 = (bf16[2048,512]{1,0:T(8,128)(2,1)S(1)}, bf16[2048,512]{1,0:T(8,128)(2,1)}, u32[]{:S(2)}) copy-start(bf16[2048,512]{1,0:T(8,128)(2,1)} %refs_2_.11) | copy-start | bytes 6291460
  0.6 1.7 %copy-start.2 = (bf16[2048,512]{1,0:T(8,128)(2,1)S(1)}, bf16[2048,512]{1,0:T(8,128)(2,1)}, u32[]{:S(2)}) copy-start(bf16[2048,512]{1,0:T(8,128)(2,1)} %table_ref.1) | copy-start | bytes 6291460
  2.4 0.7 copy-start.4
  3.0 0.7 copy-start.5
  4.3 9.5 %collective-permute-start.8 = (bf16[144,512]{1,0:T(8,128)(2,1)S(1)}, bf16[144,512]{1,0:T(8,128)(2,1)S(1)}, u32[]{:S(2)}, u32[]{:S(2)}) collective-permute-start(bf16[144,512]{1,0:T(8,128)(2,1)S(1)} %gather.1.refs_0_), channel_id=1, source_target_pairs={{0,2},{1,3},{2,0},{3,1},{4,6},{5,7},{6,4},{7,5},{8,10},{9,11},{10,... | collective-permute-start | bytes 442376 | tf_op jit(solution)/shard_map/ppermute | solution.py:189
  7.4 9.4 %collective-permute-start = (bf16[144,512]{1,0:T(8,128)(2,1)S(1)}, bf16[144,512]{1,0:T(8,128)(2,1)S(1)}, u32[]{:S(2)}, u32[]{:S(2)}) collective-permute-start(bf16[144,512]{1,0:T(8,128)(2,1)S(1)} %gather.1.refs_0_), channel_id=1, source_target_pairs={{0,4},{1,5},{2,6},{3,7},{4,0},{5,1},{6,2},{7,3},{8,12},{9,13},{10,... | collective-permute-start | bytes 442376 | tf_op jit(solution)/shard_map/ppermute | solution.py:189
  13.8 9.7 %collective-permute-start.9 = (bf16[288,512]{1,0:T(8,128)(2,1)S(1)}, bf16[288,512]{1,0:T(8,128)(2,1)S(1)}, u32[]{:S(2)}, u32[]{:S(2)}) collective-permute-start(bf16[288,512]{1,0:T(8,128)(2,1)S(1)} %pad_maximum_fusion), channel_id=1, source_target_pairs={{0,16},{1,17},{2,18},{3,19},{4,20},{5,21},{6,22},{7,23},{8,9},{9,8... | collective-permute-start | bytes 884744 | tf_op jit(solution)/shard_map/ppermute | solution.py:189
  16.8 5.1 %collective-permute-start.1 = (bf16[144,512]{1,0:T(8,128)(2,1)S(1)}, bf16[144,512]{1,0:T(8,128)(2,1)S(1)}, u32[]{:S(2)}, u32[]{:S(2)}) collective-permute-start(bf16[144,512]{1,0:T(8,128)(2,1)S(1)} %collective-permute-done.refs_0_), channel_id=1, source_target_pairs={{0,2},{1,3},{2,0},{3,1},{4,6},{5,7},{6,4},{7,5},{8,10},{9,11},{10,... | collective-permute-start | bytes 442376 | tf_op jit(solution)/shard_map/ppermute | solution.py:189
  17.2 4.7 %collective-permute-start.18 = (bf16[144,512]{1,0:T(8,128)(2,1)S(1)}, bf16[144,512]{1,0:T(8,128)(2,1)S(1)}, u32[]{:S(2)}, u32[]{:S(2)}) collective-permute-start(bf16[144,512]{1,0:T(8,128)(2,1)S(1)} %gather.1.refs_0_), channel_id=1, source_target_pairs={{0,8},{1,9},{2,10},{3,11},{4,12},{5,13},{6,14},{7,15},{8,0},{9,1},... | collective-permute-start | bytes 442376 | tf_op jit(solution)/shard_map/ppermute | solution.py:189
  17.2 17.5 %collective-permute-start.12 = (bf16[288,512]{1,0:T(8,128)(2,1)S(1)}, bf16[288,512]{1,0:T(8,128)(2,1)S(1)}, u32[]{:S(2)}, u32[]{:S(2)}) collective-permute-start(bf16[288,512]{1,0:T(8,128)(2,1)S(1)} %pad_maximum_fusion), channel_id=1, source_target_pairs={{0,1},{1,0},{2,3},{3,2},{4,5},{5,4},{6,7},{7,6},{8,24},{9,25},{10,... | collective-permute-start | bytes 884744 | tf_op jit(solution)/shard_map/ppermute | solution.py:189
  18.8 9.0 %collective-permute-start.17 = (bf16[144,512]{1,0:T(8,128)(2,1)S(1)}, bf16[144,512]{1,0:T(8,128)(2,1)S(1)}, u32[]{:S(2)}, u32[]{:S(2)}) collective-permute-start(bf16[144,512]{1,0:T(8,128)(2,1)S(1)} %collective-permute-done.8.refs_0_), channel_id=1, source_target_pairs={{0,8},{1,9},{2,10},{3,11},{4,12},{5,13},{6,14},{7,15},{8,0},{9,1},... | collective-permute-start | bytes 442376 | tf_op jit(solution)/shard_map/ppermute | solution.py:189
  21.9 12.0 %collective-permute-start.16 = (bf16[144,512]{1,0:T(8,128)(2,1)S(1)}, bf16[144,512]{1,0:T(8,128)(2,1)S(1)}, u32[]{:S(2)}, u32[]{:S(2)}) collective-permute-start(bf16[144,512]{1,0:T(8,128)(2,1)S(1)} %collective-permute-done.refs_0_), channel_id=1, source_target_pairs={{0,8},{1,9},{2,10},{3,11},{4,12},{5,13},{6,14},{7,15},{8,0},{9,1},... | collective-permute-start | bytes 442376 | tf_op jit(solution)/shard_map/ppermute | solution.py:189
  22.0 17.6 %collective-permute-start.2 = (bf16[288,512]{1,0:T(8,128)(2,1)S(1)}, bf16[288,512]{1,0:T(8,128)(2,1)S(1)}, u32[]{:S(2)}, u32[]{:S(2)}) collective-permute-start(bf16[288,512]{1,0:T(8,128)(2,1)S(1)} %constant_dynamic-update-slice_fusion), channel_id=1, source_target_pairs={{0,16},{1,17},{2,18},{3,19},{4,20},{5,21},{6,22},{7,23},{8,9},{9,8... | collective-permute-start | bytes 884744 | tf_op jit(solution)/shard_map/ppermute | solution.py:189
  23.5 16.6 %collective-permute-start.15 = (bf16[288,512]{1,0:T(8,128)(2,1)S(1)}, bf16[288,512]{1,0:T(8,128)(2,1)S(1)}, u32[]{:S(2)}, u32[]{:S(2)}) collective-permute-start(bf16[288,512]{1,0:T(8,128)(2,1)S(1)} %collective-permute-done.9.refs_0_), channel_id=1, source_target_pairs={{0,8},{1,9},{2,10},{3,11},{4,12},{5,13},{6,14},{7,15},{8,0},{9,1},... | collective-permute-start | bytes 884744 | tf_op jit(solution)/shard_map/ppermute | solution.py:189
  23.8 1.6 %copy-start = (bf16[2048,512]{1,0:T(8,128)(2,1)S(1)}, bf16[2048,512]{1,0:T(8,128)(2,1)}, u32[]{:S(2)}) copy-start(bf16[2048,512]{1,0:T(8,128)(2,1)} %refs_2_.11) | copy-start | bytes 6291460
  27.8 18.9 %collective-permute-start.6 = (bf16[288,512]{1,0:T(8,128)(2,1)S(1)}, bf16[288,512]{1,0:T(8,128)(2,1)S(1)}, u32[]{:S(2)}, u32[]{:S(2)}) collective-permute-start(bf16[288,512]{1,0:T(8,128)(2,1)S(1)} %constant_dynamic-update-slice_fusion), channel_id=1, source_target_pairs={{0,1},{1,0},{2,3},{3,2},{4,5},{5,4},{6,7},{7,6},{8,24},{9,25},{10,... | collective-permute-start | bytes 884744 | tf_op jit(solution)/shard_map/ppermute | solution.py:189
  33.9 13.2 %collective-permute-start.10 = (bf16[288,512]{1,0:T(8,128)(2,1)S(1)}, bf16[288,512]{1,0:T(8,128)(2,1)S(1)}, u32[]{:S(2)}, u32[]{:S(2)}) collective-permute-start(bf16[288,512]{1,0:T(8,128)(2,1)S(1)} %collective-permute-done.9.refs_0_), channel_id=1, source_target_pairs={{0,1},{1,0},{2,3},{3,2},{4,5},{5,4},{6,7},{7,6},{8,24},{9,25},{10,... | collective-permute-start | bytes 884744 | tf_op jit(solution)/shard_map/ppermute | solution.py:189
  34.8 12.5 %collective-permute-start.13 = (bf16[288,512]{1,0:T(8,128)(2,1)S(1)}, bf16[288,512]{1,0:T(8,128)(2,1)S(1)}, u32[]{:S(2)}, u32[]{:S(2)}) collective-permute-start(bf16[288,512]{1,0:T(8,128)(2,1)S(1)} %collective-permute-done.12.refs_0_), channel_id=1, source_target_pairs={{0,8},{1,9},{2,10},{3,11},{4,12},{5,13},{6,14},{7,15},{8,0},{9,1},... | collective-permute-start | bytes 884744 | tf_op jit(solution)/shard_map/ppermute | solution.py:189
  39.5 5.9 %collective-permute-start.14 = (bf16[144,512]{1,0:T(8,128)(2,1)S(1)}, bf16[144,512]{1,0:T(8,128)(2,1)S(1)}, u32[]{:S(2)}, u32[]{:S(2)}) collective-permute-start(bf16[144,512]{1,0:T(8,128)(2,1)S(1)} %collective-permute-done.1.refs_2_), channel_id=1, source_target_pairs={{0,8},{1,9},{2,10},{3,11},{4,12},{5,13},{6,14},{7,15},{8,0},{9,1},... | collective-permute-start | bytes 442376 | tf_op jit(solution)/shard_map/ppermute | solution.py:189
  40.1 21.7 %collective-permute-start.5 = (bf16[288,512]{1,0:T(8,128)(2,1)S(1)}, bf16[288,512]{1,0:T(8,128)(2,1)S(1)}, u32[]{:S(2)}, u32[]{:S(2)}) collective-permute-start(bf16[288,512]{1,0:T(8,128)(2,1)S(1)} %collective-permute-done.2.refs_0_), channel_id=1, source_target_pairs={{0,8},{1,9},{2,10},{3,11},{4,12},{5,13},{6,14},{7,15},{8,0},{9,1},... | collective-permute-start | bytes 884744 | tf_op jit(solution)/shard_map/ppermute | solution.py:189
  45.4 10.5 %collective-permute-start.3 = (bf16[288,512]{1,0:T(8,128)(2,1)S(1)}, bf16[288,512]{1,0:T(8,128)(2,1)S(1)}, u32[]{:S(2)}, u32[]{:S(2)}) collective-permute-start(bf16[288,512]{1,0:T(8,128)(2,1)S(1)} %collective-permute-done.2.refs_0_), channel_id=1, source_target_pairs={{0,1},{1,0},{2,3},{3,2},{4,5},{5,4},{6,7},{7,6},{8,24},{9,25},{10,... | collective-permute-start | bytes 884744 | tf_op jit(solution)/shard_map/ppermute | solution.py:189
  46.8 15.0 %collective-permute-start.7 = (bf16[288,512]{1,0:T(8,128)(2,1)S(1)}, bf16[288,512]{1,0:T(8,128)(2,1)S(1)}, u32[]{:S(2)}, u32[]{:S(2)}) collective-permute-start(bf16[288,512]{1,0:T(8,128)(2,1)S(1)} %collective-permute-done.6.refs_2_), channel_id=1, source_target_pairs={{0,8},{1,9},{2,10},{3,11},{4,12},{5,13},{6,14},{7,15},{8,0},{9,1},... | collective-permute-start | bytes 884744 | tf_op jit(solution)/shard_map/ppermute | solution.py:189
  47.1 9.3 %collective-permute-start.11 = (bf16[288,512]{1,0:T(8,128)(2,1)S(1)}, bf16[288,512]{1,0:T(8,128)(2,1)S(1)}, u32[]{:S(2)}, u32[]{:S(2)}) collective-permute-start(bf16[288,512]{1,0:T(8,128)(2,1)S(1)} %collective-permute-done.10.refs_0_), channel_id=1, source_target_pairs={{0,8},{1,9},{2,10},{3,11},{4,12},{5,13},{6,14},{7,15},{8,0},{9,1},... | collective-permute-start | bytes 884744 | tf_op jit(solution)/shard_map/ppermute | solution.py:189
  56.0 14.8 %collective-permute-start.4 = (bf16[288,512]{1,0:T(8,128)(2,1)S(1)}, bf16[288,512]{1,0:T(8,128)(2,1)S(1)}, u32[]{:S(2)}, u32[]{:S(2)}) collective-permute-start(bf16[288,512]{1,0:T(8,128)(2,1)S(1)} %collective-permute-done.3.refs_0_), channel_id=1, source_target_pairs={{0,8},{1,9},{2,10},{3,11},{4,12},{5,13},{6,14},{7,15},{8,0},{9,1},... | collective-permute-start | bytes 884744 | tf_op jit(solution)/shard_map/ppermute | solution.py:189
  61.8 8.9 %copy-start.3 = (f32[2048]{0:T(1024)S(1)}, f32[2048]{0:T(1024)}, u32[]{:S(2)}) copy-start(f32[2048]{0:T(1024)} %param.9) | copy-start | bytes 24580

commit v2 on v1

v2 whole, which is shorter than its diff:
```python
import functools
import math

import jax
import jax.numpy as jnp
from jax import lax
from jax.experimental import pallas as pl
from jax.experimental.pallas import tpu as pltpu
from jax.sharding import PartitionSpec as P

BF16, F32 = jnp.bfloat16, jnp.float32
AXES = ("blk", "grp")
EXTRA = 16
LANES = 128
VMEM = pl.BlockSpec(memory_space=pltpu.VMEM)
NT = (((1,), (1,)), ((), ()))


def in_vmem(array):
    return pltpu.with_memory_space_constraint(array, pltpu.VMEM)


def eye():
    shape = (LANES, LANES)
    return lax.broadcasted_iota(jnp.int32, shape, 0) == lax.broadcasted_iota(jnp.int32, shape, 1)


def to_row(column):
    return jnp.sum(jnp.where(eye(), column, 0.0), axis=0, keepdims=True)


def to_column(row):
    return jnp.sum(jnp.where(eye(), row, 0.0), axis=1, keepdims=True)


def gather_kernel(table_ref, ids_ref, pots_ref, out_ref, held_ref, ids_held, pots_held, sems):
    records, width = table_ref.shape
    count = ids_ref.shape[1]
    step = 512
    parts = [pl.ds(first, step) for first in range(0, records, step)]
    copies = [pltpu.make_async_copy(ids_ref, ids_held, sems.at[0]), pltpu.make_async_copy(pots_ref, pots_held, sems.at[1])]
    copies += [pltpu.make_async_copy(table_ref.at[p, :], held_ref.at[p, :], sems.at[i + 2]) for i, p in enumerate(parts)]
    for copy in copies:
        copy.start()
    copies[0].wait()
    column = to_column(ids_held[...].astype(F32)).astype(jnp.int32)
    rows = jnp.zeros((count, width), F32)
    for i, copy in enumerate(copies[2:]):
        spot = lax.broadcasted_iota(jnp.int32, (count, step), 1) + i * step
        pick = jnp.where(spot == column, 1.0, 0.0).astype(BF16)
        copy.wait()
        rows += jnp.dot(pick, held_ref[i * step : (i + 1) * step, :], preferred_element_type=F32)
    norm = to_row(jnp.sum(jnp.square(rows), axis=1, keepdims=True))
    copies[1].wait()
    term = pots_held[...].astype(F32) * (width / 2) - 0.5 * norm
    high = term.astype(BF16).astype(F32)
    middle = (term - high).astype(BF16).astype(F32)
    low = term - high - middle
    line = lax.broadcasted_iota(jnp.int32, (EXTRA, LANES), 0)
    split = jnp.where(line == 0, high, jnp.where(line == 1, middle, jnp.where(line == 2, low, 0.0)))
    out_ref[0:count, :] = rows.astype(BF16)
    out_ref[count:, :] = jnp.zeros((EXTRA, width), BF16)
    out_ref[count:, 0:LANES] = split.astype(BF16)


def gather(table, row_ids, potentials):
    count, (records, width) = row_ids.shape[0], table.shape
    args = [table, row_ids.reshape(1, count), potentials.reshape(1, count)]
    return pl.pallas_call(
        gather_kernel,
        out_shape=pltpu.VMEM((count + EXTRA, width), BF16),
        in_specs=[pl.BlockSpec(memory_space=pltpu.HBM)] * 3,
        out_specs=VMEM,
        scratch_shapes=[
            pltpu.VMEM((records, width), BF16),
            pltpu.VMEM((1, count), jnp.int32),
            pltpu.VMEM((1, count), BF16),
            pltpu.SemaphoreType.DMA((records // 512 + 2,)),
        ],
        compiler_params=pltpu.CompilerParams(vmem_limit_bytes=16 << 20),
        name="gather",
    )(*[pltpu.with_memory_space_constraint(a, pltpu.HBM) for a in args])


def pieces(refs, count):
    rows, terms = [], []
    for ref in refs:
        for first in range(0, ref.shape[0], count + EXTRA):
            rows.append(ref[first : first + count, :])
            extra = ref[first + count : first + count + EXTRA, 0:LANES].astype(F32)
            terms.append(jnp.sum(extra, axis=0, keepdims=True))
    return rows, terms


BLOCK=512
def visit_kernel(shards, count, block, chunk, first, last, scale, *refs):
    shard_refs, refs = refs[:shards], refs[shards:]
    centres_ref, refs = refs[0], refs[1:]
    if first:
        source_ref, centres_ref, load_sems, refs = centres_ref, refs[-2], refs[-1], refs[:-2]
    state_in, refs = (None, refs) if first else (refs[:3], refs[3:])
    if last:
        (centre_ref, balance_ref), refs = refs[:2], refs[2:]
        means_ref, potential_ref, held_ref, sems = refs
    width = centres_ref.shape[1]
    alpha = math.log2(math.e) * 2.0 * scale / width
    rows, terms = pieces(shard_refs, count)
    per = max(1, chunk // count)
    groups = [
        (jnp.concatenate(rows[i : i + per], axis=0), jnp.concatenate(terms[i : i + per], axis=1))
        for i in range(0, len(rows), per)
    ]
    acc_ref = held_ref if last else refs[2]


    total = centres_ref.shape[0]
    units = [(j, g) for j in range(total // block) for g in range(len(groups))]
    carry = {}

    def scores(u):
        j, g = u
        at = slice(j * block, (j + 1) * block)
        return lax.dot_general(centres_ref[at, :], groups[g][0], NT, preferred_element_type=F32) + groups[g][1]

    def soft(u, shifted):
        j, g = u
        at = slice(j * block, (j + 1) * block)
        if g == 0:
            old = None if first else state_in[0][at, :]
            mass = None if first else state_in[1][at, :]
        else:
            old, mass = carry[j]
        lanes = [slice(f, f + LANES) for f in range(0, shifted.shape[1], LANES)]
        top = jnp.broadcast_to(jnp.max(shifted, axis=1, keepdims=True), (block, LANES))
        shrink = None
        if old is not None:
            top = jnp.maximum(old, top)
            shrink = jnp.exp2((old - top) * alpha)
            mass = mass * shrink
        parts = []
        for lane in lanes:
            expd = jnp.exp2((shifted[:, lane] - top) * alpha)
            mass = expd if mass is None else mass + expd
            parts.append(expd.astype(BF16))
        carry[j] = (top, mass)
        return jnp.concatenate(parts, axis=1), shrink

    def weigh(u, expd, shrink):
        j, g = u
        at = slice(j * block, (j + 1) * block)
        numer = jnp.dot(expd, groups[g][0], preferred_element_type=F32)
        acc_in = acc_ref if g else (None if first else state_in[2])
        done = g == len(groups) - 1
        if done:
            top, mass = carry[j]
            if last:
                total_mass = jnp.broadcast_to(jnp.sum(mass, axis=1, keepdims=True), (block, LANES))
                inverse = 1.0 / total_mass
                for i in range(block // LANES):
                    part = slice(i * LANES, (i + 1) * LANES)
                    k = j * (block // LANES) + i
                    line = slice(k, k + 1)
                    peak = (scale / width) * (2.0 * to_row(top[part]) - centre_ref[line, :])
                    potential_ref[line, :] = (
                        jnp.log(balance_ref[line, :]) - peak - jnp.log(to_row(total_mass[part]))
                    ) / scale
            else:
                if j == 0:
                    refs[3][...] = top[0:8, :]
                refs[0][at, :] = top
                refs[1][at, :] = mass
        for f in range(0, width, LANES):
            lane = slice(f, f + LANES)
            value = numer[:, lane]
            if acc_in is not None:
                value = acc_in[at, lane] * shrink + value
            if done and last:
                value = value * inverse
            acc_ref[at, lane] = value
        if done and last:
            out_copy(j).start()

    def out_copy(j):
        at = pl.ds(j * block, block)
        return pltpu.make_async_copy(held_ref.at[at, :], means_ref.at[at, :], sems.at[j])

    def load(j):
        at = pl.ds(j * block, block)
        return pltpu.make_async_copy(source_ref.at[at, :], centres_ref.at[at, :], load_sems.at[j])

    if first:
        for j in range(total // block):
            load(j).start()
        for j in range(total // block):
            load(j).wait()
        for i in range(total // LANES):
            centre = jnp.sum(jnp.square(centres_ref[i * LANES : (i + 1) * LANES, :].astype(F32)), axis=1, keepdims=True)
            refs[4][i : i + 1, :] = to_row(centre)

    ahead = scores(units[0])
    for i, u in enumerate(units):
        now = ahead
        if i + 1 < len(units):
            ahead = scores(units[i + 1])
        weigh(u, *soft(u, now))
    if last:
        for j in range(total // block):
            out_copy(j).wait()


def visit(shards, count, centroids, state, scale, balance=None, chunk=1024, cost=0.4):
    total, width = centroids.shape
    block = min(1024, total)
    first, last = state is None, balance is not None
    number = sum(s.shape[0] // (count + EXTRA) for s in shards)
    lines = (total // LANES, LANES)
    scratch = []
    if last:
        out_shape = [jax.ShapeDtypeStruct((total, width), F32), jax.ShapeDtypeStruct(lines, F32)]
        out_specs = [pl.BlockSpec(memory_space=pltpu.HBM), VMEM]
        scratch = [pltpu.VMEM((total, width), F32), pltpu.SemaphoreType.DMA((total // block,))]
    else:
        shapes = [(total, LANES), (total, LANES), (total, width), (8, LANES)] + ([lines] if first else [])
        out_shape = [pltpu.VMEM(shape, F32) for shape in shapes]
        if first:
            out_shape.append(pltpu.VMEM((total, width), BF16))
            scratch = [pltpu.SemaphoreType.DMA((total // block,))]
        out_specs = [VMEM] * len(out_shape)
    args = [in_vmem(s) for s in shards]
    args.append(pltpu.with_memory_space_constraint(centroids, pltpu.HBM) if first else in_vmem(state[5]))
    aliases = {}
    if not first:
        if not last:
            aliases = {len(args) + i: i for i in range(3)}
        args += [in_vmem(s) for s in state[:3]]
    if last:
        args += [in_vmem(state[4]), balance.reshape(lines)]
    rows = number * count
    out = pl.pallas_call(
        functools.partial(visit_kernel, len(shards), count, block, chunk, first, last, scale),
        out_shape=tuple(out_shape),
        in_specs=[pl.BlockSpec(memory_space=pltpu.HBM) if first and i == len(shards) else VMEM for i in range(len(args))],
        out_specs=tuple(out_specs),
        scratch_shapes=scratch,
        input_output_aliases=aliases,
        compiler_params=pltpu.CompilerParams(vmem_limit_bytes=40 << 20),
        cost_estimate=pl.CostEstimate(flops=int(cost * 4 * rows * total * width), bytes_accessed=1024, transcendentals=0),
        name="visit",
    )(*args)
    return out if first or last else (*out, *state[4:])


def joined_kernel(*refs):
    out_ref, first = refs[-1], 0
    for ref in refs[1:-1]:
        out_ref[first : first + ref.shape[0], :] = ref[...]
        first += ref.shape[0]


def joined(parts, token):
    rows = sum(p.shape[0] for p in parts)
    return pl.pallas_call(
        joined_kernel,
        out_shape=pltpu.VMEM((rows, parts[0].shape[1]), BF16),
        in_specs=[VMEM] * (len(parts) + 1),
        out_specs=VMEM,
        compiler_params=pltpu.CompilerParams(vmem_limit_bytes=16 << 20),
        cost_estimate=pl.CostEstimate(flops=0, bytes_accessed=0, transcendentals=0),
        name="joined",
    )(in_vmem(token), *[in_vmem(p) for p in parts])


def body(table, row_ids, potentials, centroids, balance):
    scale = 1.5 * math.sqrt(table.shape[1])
    count = row_ids.shape[0]
    blk, grp = lax.axis_size("blk"), lax.axis_size("grp")

    def swap(array, flip):
        route = [(i, flip(i // grp, i % grp)) for i in range(blk * grp)]
        return lax.ppermute(array, AXES, route)

    def core(array):
        return swap(array, lambda b, g: (b ^ 1) * grp + g)

    def grp_bit(array, bit):
        return swap(array, lambda b, g: b * grp + (g ^ bit))

    def one_way(array):
        return swap(array, lambda b, g: b * grp + (g ^ 1) if b & 1 else (b ^ 2) * grp + g)

    def other_way(array):
        return swap(array, lambda b, g: (b ^ 2) * grp + g if b & 1 else b * grp + (g ^ 1))

    own = gather(table, row_ids, potentials)
    bit = grp // 2
    while bit > 4:
        own = jnp.concatenate([own, grp_bit(own, bit)], axis=0)
        bit //= 2
    look = functools.partial(visit, count=count, centroids=centroids, scale=scale)
    far = grp_bit(own, 4)
    near = grp_bit(own, 2)
    state = look([own, core(own)], state=None, cost=0.01)
    t = state[3]
    a = one_way(joined([own], t))
    near_core = core(joined([near], t))
    two = joined([near, far], t)
    a_two = one_way(two)
    both = grp_bit(joined([far], t), 2)
    far_core = core(joined([far], t))
    state = look([near, far, near_core, far_core], state=state)
    t = state[3]
    b = other_way(joined([own, a], t))
    b_four = other_way(joined([two, a_two], t))
    a_both = one_way(joined([both], t))
    second_core = core(joined([a, a_two, both], t))
    state = look([a, a_two, both, second_core], state=state)
    t = state[3]
    b_two = other_way(joined([both, a_both], t))
    third_core = core(joined([b, a_both], t))
    state = look([b, a_both, third_core], state=state)
    t = state[3]
    b_four_core = core(joined([b_four], t))
    b_two_core = core(joined([b_two], t))
    state = look([b_four, b_two], state=state)
    means, potential = look([b_four_core, b_two_core], state=state, balance=balance)
    return means, potential.reshape(balance.shape)


def solution(mesh):
    placed = (
        P(AXES, None),
        P(AXES),
        P(AXES),
        P(AXES, None),
        P(AXES),
    )
    return jax.shard_map(
        body,
        mesh=mesh,
        in_specs=placed,
        out_specs=(P(AXES, None), P(AXES)),
        check_vma=False,
    )
```

time: 79.3 us -> 53.1 us (0.67)
  Pallas kernels: 49 us -> 30.5 us
  local copies, waits for them, and re-layouts: 4.67 us -> 0.01 us
  waiting for transfers between devices: 7.92 us -> 6.07 us
  starting transfers between devices: 16.6 us -> 15.3 us
    pallas_call x8 -> x6, Pallas kernels: 48.4 us -> 28.2 us  [visit(): pl.pallas_call(functools.partial(visit_kernel, len(shards), count, block,...]
    unnamed x13 -> x2, local copies, waits for them, and re-layouts: 4.66 us -> 0.01 us
    ppermute x19 -> x16, waiting for transfers between devices: 7.92 us -> 6.07 us  [swap(): return lax.ppermute(array, AXES, route)]
    pallas_call x1, Pallas kernels: 0.59 us -> 1.94 us  [gather(): pl.pallas_call(gather_kernel, out_shape=pltpu.VMEM((count + EXTRA, width)...]
    ppermute x19 -> x16, starting transfers between devices: 16.6 us -> 15.3 us  [swap(): return lax.ppermute(array, AXES, route)]
  transfers between devices with their start and end apart: 19 -> 16, of which waited for: 3 -> 6; matrix products, arithmetic and copies ran while one was open for 0% -> 0% of each run, Pallas kernels for 51% -> 42%
where the time goes in v2:
time: 53.1 us; the launch traced here: 52.8 us
  Pallas kernels  30.5 us (57%)
  starting transfers between devices  15.3 us (29%)
  waiting for transfers between devices  6.07 us (11%)
  between operations  0.98 us (2%)
    pallas_call x6, Pallas kernels, visit(): pl.pallas_call(functools.partial(visit_kernel, len(shards), count, block,...  28.2 us
    ppermute x16, starting transfers between devices, swap(): return lax.ppermute(array, AXES, route)  15.3 us
    ppermute x16, waiting for transfers between devices, swap(): return lax.ppermute(array, AXES, route)  6.07 us
    pallas_call x1, Pallas kernels, gather(): pl.pallas_call(gather_kernel, out_shape=pltpu.VMEM((count + EXTRA, width)...  1.94 us
  transfers between devices with their start and end apart: 16, of which 6 were waited for; matrix products, arithmetic and copies ran while one was open for 0% of the time, Pallas kernels for 42%

profile of v2, /device:TPU:0, one launch (start us, length us, event | category | flops | bytes accessed | tf_op | source)
XLA Modules:
  0.0 52.8 jit_solution(5046231671063529442)
XLA Ops:
  0.6 1.9 %gather.1.refs_0_.refs_1_ = bf16[144,512]{1,0:T(8,128)(2,1)S(1)} custom-call(bf16[2048,512]{1,0:T(8,128)(2,1)} %table_ref.1, s32[1,128]{1,0:T(1,128)} %bitcast.5, bf16[1,128]{1,0:T(2,128)(2,1)} %bitcast.6), custom_call_target="tpu_custom_call" | custom-call | tf_op jit(solution)/shard_map/gather/pallas_call | solution.py:69
  2.6 0.5 collective-permute-start.2
  3.1 3.7 %collective-permute-start.1 = (bf16[144,512]{1,0:T(8,128)(2,1)S(1)}, bf16[144,512]{1,0:T(8,128)(2,1)S(1)}, u32[]{:S(2)}, u32[]{:S(2)}) collective-permute-start(bf16[144,512]{1,0:T(8,128)(2,1)S(1)} %gather.1.refs_0_.refs_1_), channel_id=1, source_target_pairs={{0,4},{1,5},{2,6},{3,7},{4,0},{5,1},{6,2},{7,3},{8,12},{9,13},{10,... | collective-permute-start | bytes 442376 | tf_op jit(solution)/shard_map/ppermute | solution.py:280
  6.8 1.6 %collective-permute-start = (bf16[144,512]{1,0:T(8,128)(2,1)S(1)}, bf16[144,512]{1,0:T(8,128)(2,1)S(1)}, u32[]{:S(2)}, u32[]{:S(2)}) collective-permute-start(bf16[144,512]{1,0:T(8,128)(2,1)S(1)} %gather.1.refs_0_.refs_1_), channel_id=1, source_target_pairs={{0,2},{1,3},{2,0},{3,1},{4,6},{5,7},{6,4},{7,5},{8,10},{9,11},{10,... | collective-permute-start | bytes 442376 | tf_op jit(solution)/shard_map/ppermute | solution.py:280
  8.3 0.0 collective-permute-done.2.refs_1_
  8.3 3.1 %visit.6 = (f32[2048,128]{1,0:T(8,128)S(1)}, f32[2048,128]{1,0:T(8,128)S(1)}, f32[2048,512]{1,0:T(8,128)S(1)}, f32[8,128]{1,0:T(8,128)S(1)}, f32[16,128]{1,0:T(8,128)S(1)}, /*index=5*/bf16[2048,512]{1,0:T(8,128)(2,1)S(1)}) custom-call(bf16[144,512]{1,0:T(8,128)(2,1)S(1)} %gather.1.refs_0_.refs_1_, bf16[144,512]{1,0:T(8,128)(2,1)S(1)} %collective-permute-done.2.refs_1_, ...), custom_call_target="tpu_custom_call" | custom-call | flops 10737418 | bytes 1024 | tf_op jit(solution)/shard_map/visit/pallas_call | solution.py:239
  11.4 3.0 %collective-permute-done.1.refs_1_.refs_2_ = bf16[144,512]{1,0:T(8,128)(2,1)S(1)} collective-permute-done((bf16[144,512]{1,0:T(8,128)(2,1)S(1)}, bf16[144,512]{1,0:T(8,128)(2,1)S(1)}, u32[]{:S(2)}, u32[]{:S(2)}) %collective-permute-start.1) | collective-permute-done | bytes 147488 | tf_op jit(solution)/shard_map/ppermute | solution.py:280
  14.5 0.2 collective-permute-done.refs_1_.refs_0_
  14.7 1.6 %collective-permute-start.9 = (bf16[288,512]{1,0:T(8,128)(2,1)S(1)}, bf16[288,512]{1,0:T(8,128)(2,1)S(1)}, u32[]{:S(2)}, u32[]{:S(2)}) collective-permute-start(bf16[288,512]{1,0:T(8,128)(2,1)S(1)} %joined.17.refs_1_), channel_id=1, source_target_pairs={{0,16},{1,17},{2,18},{3,19},{4,20},{5,21},{6,22},{7,23},{8,9},{9,8... | collective-permute-start | bytes 884744 | tf_op jit(solution)/shard_map/ppermute | solution.py:280
  16.3 0.1 collective-permute-start.4
  16.4 0.6 %collective-permute-start.3 = (bf16[144,512]{1,0:T(8,128)(2,1)S(1)}, bf16[144,512]{1,0:T(8,128)(2,1)S(1)}, u32[]{:S(2)}, u32[]{:S(2)}) collective-permute-start(bf16[144,512]{1,0:T(8,128)(2,1)S(1)} %joined.12), channel_id=1, source_target_pairs={{0,8},{1,9},{2,10},{3,11},{4,12},{5,13},{6,14},{7,15},{8,0},{9,1},... | collective-permute-start | bytes 442376 | tf_op jit(solution)/shard_map/ppermute | solution.py:280
  17.0 1.4 %collective-permute-start.7 = (bf16[144,512]{1,0:T(8,128)(2,1)S(1)}, bf16[144,512]{1,0:T(8,128)(2,1)S(1)}, u32[]{:S(2)}, u32[]{:S(2)}) collective-permute-start(bf16[144,512]{1,0:T(8,128)(2,1)S(1)} %joined.13), channel_id=1, source_target_pairs={{0,2},{1,3},{2,0},{3,1},{4,6},{5,7},{6,4},{7,5},{8,10},{9,11},{10,... | collective-permute-start | bytes 442376 | tf_op jit(solution)/shard_map/ppermute | solution.py:280
  18.4 0.6 %collective-permute-start.5 = (bf16[144,512]{1,0:T(8,128)(2,1)S(1)}, bf16[144,512]{1,0:T(8,128)(2,1)S(1)}, u32[]{:S(2)}, u32[]{:S(2)}) collective-permute-start(bf16[144,512]{1,0:T(8,128)(2,1)S(1)} %joined.14), channel_id=1, source_target_pairs={{0,16},{1,17},{2,18},{3,19},{4,20},{5,21},{6,22},{7,23},{8,9},{9,8... | collective-permute-start | bytes 442376 | tf_op jit(solution)/shard_map/ppermute | solution.py:280
  19.0 0.0 collective-permute-done.4.refs_3_
  19.0 0.0 collective-permute-done.3.refs_2_
  19.0 3.4 %visit.7 = (f32[2048,128]{1,0:T(8,128)S(1)}, f32[2048,128]{1,0:T(8,128)S(1)}, f32[2048,512]{1,0:T(8,128)S(1)}, f32[8,128]{1,0:T(8,128)S(1)}) custom-call(bf16[144,512]{1,0:T(8,128)(2,1)S(1)} %collective-permute-done.refs_1_.refs_0_, ...), custom_call_target="tpu_custom_call", output_to_operand_aliasing={{0}: (5, {}), {1}: (6, {}), {2}: (7, {})} | custom-call | flops 858993472 | bytes 1024 | tf_op jit(solution)/shard_map/visit/pallas_call | solution.py:239
  22.4 0.4 collective-permute-done.7.refs_1_.refs_3_.refs_2_
  22.8 0.8 %collective-permute-done.5.refs_2_.refs_1_.refs_0_ = bf16[144,512]{1,0:T(8,128)(2,1)S(1)} collective-permute-done((bf16[144,512]{1,0:T(8,128)(2,1)S(1)}, bf16[144,512]{1,0:T(8,128)(2,1)S(1)}, u32[]{:S(2)}, u32[]{:S(2)}) %collective-permute-start.5) | collective-permute-done | bytes 147488 | tf_op jit(solution)/shard_map/ppermute | solution.py:280
  23.6 0.0 collective-permute-done.9.refs_2_.refs_1_
  23.7 0.1 collective-permute-start.10
  23.8 1.6 %collective-permute-start.6 = (bf16[288,512]{1,0:T(8,128)(2,1)S(1)}, bf16[288,512]{1,0:T(8,128)(2,1)S(1)}, u32[]{:S(2)}, u32[]{:S(2)}) collective-permute-start(bf16[288,512]{1,0:T(8,128)(2,1)S(1)} %joined.15), channel_id=1, source_target_pairs={{0,1},{1,0},{2,3},{3,2},{4,5},{5,4},{6,7},{7,6},{8,24},{9,25},{10,... | collective-permute-start | bytes 884744 | tf_op jit(solution)/shard_map/ppermute | solution.py:280
  25.4 1.0 %collective-permute-start.8 = (bf16[144,512]{1,0:T(8,128)(2,1)S(1)}, bf16[144,512]{1,0:T(8,128)(2,1)S(1)}, u32[]{:S(2)}, u32[]{:S(2)}) collective-permute-start(bf16[144,512]{1,0:T(8,128)(2,1)S(1)} %joined.16), channel_id=1, source_target_pairs={{0,16},{1,17},{2,18},{3,19},{4,20},{5,21},{6,22},{7,23},{8,9},{9,8... | collective-permute-start | bytes 442376 | tf_op jit(solution)/shard_map/ppermute | solution.py:280
  26.5 0.6 %collective-permute-start.12 = (bf16[576,512]{1,0:T(8,128)(2,1)S(1)}, bf16[576,512]{1,0:T(8,128)(2,1)S(1)}, u32[]{:S(2)}, u32[]{:S(2)}) collective-permute-start(bf16[576,512]{1,0:T(8,128)(2,1)S(1)} %joined.20), channel_id=1, source_target_pairs={{0,1},{1,0},{2,3},{3,2},{4,5},{5,4},{6,7},{7,6},{8,24},{9,25},{10,... | collective-permute-start | bytes 1769480 | tf_op jit(solution)/shard_map/ppermute | solution.py:280
  27.0 0.0 collective-permute-done.10.refs_3_
  27.0 6.0 %visit.8 = (f32[2048,128]{1,0:T(8,128)S(1)}, f32[2048,128]{1,0:T(8,128)S(1)}, f32[2048,512]{1,0:T(8,128)S(1)}, f32[8,128]{1,0:T(8,128)S(1)}) custom-call(bf16[144,512]{1,0:T(8,128)(2,1)S(1)} %collective-permute-done.5.refs_2_.refs_1_.refs_0_, ...), custom_call_target="tpu_custom_call", output_to_operand_aliasing={{0}: (5, {}), {1}: (6, {}), {2}: (7, {})} | custom-call | flops 1717986944 | bytes 1024 | tf_op jit(solution)/shard_map/visit/pallas_call | solution.py:239
  33.1 0.0 collective-permute-done.8.refs_2_.refs_1_
  33.1 0.0 collective-permute-done.6.refs_1_.refs_0_
  33.1 0.3 collective-permute-start.11
  33.4 1.4 %collective-permute-start.14 = (bf16[288,512]{1,0:T(8,128)(2,1)S(1)}, bf16[288,512]{1,0:T(8,128)(2,1)S(1)}, u32[]{:S(2)}, u32[]{:S(2)}) collective-permute-start(bf16[288,512]{1,0:T(8,128)(2,1)S(1)} %joined.22), channel_id=1, source_target_pairs={{0,1},{1,0},{2,3},{3,2},{4,5},{5,4},{6,7},{7,6},{8,24},{9,25},{10,... | collective-permute-start | bytes 884744 | tf_op jit(solution)/shard_map/ppermute | solution.py:280
  34.8 0.2 collective-permute-done.11.refs_2_
  35.0 4.9 %visit.9 = (f32[2048,128]{1,0:T(8,128)S(1)}, f32[2048,128]{1,0:T(8,128)S(1)}, f32[2048,512]{1,0:T(8,128)S(1)}, f32[8,128]{1,0:T(8,128)S(1)}) custom-call(bf16[288,512]{1,0:T(8,128)(2,1)S(1)} %collective-permute-done.6.refs_1_.refs_0_, ...), custom_call_target="tpu_custom_call", output_to_operand_aliasing={{0}: (4, {}), {1}: (5, {}), {2}: (6, {})} | custom-call | flops 1288490240 | bytes 1024 | tf_op jit(solution)/shard_map/visit/pallas_call | solution.py:239
  39.9 0.0 collective-permute-done.12.refs_1_.refs_0_
  39.9 0.3 collective-permute-start.13
  40.2 1.4 %collective-permute-done.14.refs_1_ = bf16[288,512]{1,0:T(8,128)(2,1)S(1)} collective-permute-done((bf16[288,512]{1,0:T(8,128)(2,1)S(1)}, bf16[288,512]{1,0:T(8,128)(2,1)S(1)}, u32[]{:S(2)}, u32[]{:S(2)}) %collective-permute-start.14) | collective-permute-done | bytes 294944 | tf_op jit(solution)/shard_map/ppermute | solution.py:280
  41.7 0.1 collective-permute-start.15
  41.7 0.0 copy-start
  41.8 4.7 %visit.10 = (f32[2048,128]{1,0:T(8,128)S(1)}, f32[2048,128]{1,0:T(8,128)S(1)}, f32[2048,512]{1,0:T(8,128)S(1)}, f32[8,128]{1,0:T(8,128)}) custom-call(bf16[576,512]{1,0:T(8,128)(2,1)S(1)} %collective-permute-done.12.refs_1_.refs_0_, bf16[288,512]{1,0:T(8,128)(2,1)S(1)} %collective-permute-done.14.refs_1_, ...), custom_call_target="tpu_custom_call", output_to_operand_aliasing={{0}: (3, {}), {1}: (4, {}), {2}: (5, {})} | custom-call | flops 1288490240 | bytes 1024 | tf_op jit(solution)/shard_map/visit/pallas_call | solution.py:239
  46.4 0.0 collective-permute-done.15.refs_1_
  46.4 0.0 collective-permute-done.13.refs_0_
  46.5 0.0 copy-done
  46.5 6.2 %visit.11 = (f32[2048,512]{1,0:T(8,128)}, f32[16,128]{1,0:T(8,128)}) custom-call(bf16[576,512]{1,0:T(8,128)(2,1)S(1)} %collective-permute-done.13.refs_0_, bf16[288,512]{1,0:T(8,128)(2,1)S(1)} %collective-permute-done.15.refs_1_, bf16[2048,512]{1,0:T(8,128)(2,1)S(1)} %get-tuple-element.26.refs_4_.refs_3_.refs_2_, f32[2048,128]{1,0:T(8,128)S(1)} %get-tuple-element.42.refs_3_, ...), custom_call_target="tpu_custom_call" | custom-call | flops 1288490240 | bytes 1024 | tf_op jit(solution)/shard_map/visit/pallas_call | solution.py:239
  (12 shorter events, 0.3 us)
Async XLA Ops:
  2.6 5.8 %collective-permute-start.2 = (bf16[144,512]{1,0:T(8,128)(2,1)S(1)}, bf16[144,512]{1,0:T(8,128)(2,1)S(1)}, u32[]{:S(2)}, u32[]{:S(2)}) collective-permute-start(bf16[144,512]{1,0:T(8,128)(2,1)S(1)} %gather.1.refs_0_.refs_1_), channel_id=1, source_target_pairs={{0,8},{1,9},{2,10},{3,11},{4,12},{5,13},{6,14},{7,15},{8,0},{9,1},... | collective-permute-start | bytes 442376 | tf_op jit(solution)/shard_map/ppermute | solution.py:280
  3.1 11.4 %collective-permute-start.1 = (bf16[144,512]{1,0:T(8,128)(2,1)S(1)}, bf16[144,512]{1,0:T(8,128)(2,1)S(1)}, u32[]{:S(2)}, u32[]{:S(2)}) collective-permute-start(bf16[144,512]{1,0:T(8,128)(2,1)S(1)} %gather.1.refs_0_.refs_1_), channel_id=1, source_target_pairs={{0,4},{1,5},{2,6},{3,7},{4,0},{5,1},{6,2},{7,3},{8,12},{9,13},{10,... | collective-permute-start | bytes 442376 | tf_op jit(solution)/shard_map/ppermute | solution.py:280
  6.8 7.9 %collective-permute-start = (bf16[144,512]{1,0:T(8,128)(2,1)S(1)}, bf16[144,512]{1,0:T(8,128)(2,1)S(1)}, u32[]{:S(2)}, u32[]{:S(2)}) collective-permute-start(bf16[144,512]{1,0:T(8,128)(2,1)S(1)} %gather.1.refs_0_.refs_1_), channel_id=1, source_target_pairs={{0,2},{1,3},{2,0},{3,1},{4,6},{5,7},{6,4},{7,5},{8,10},{9,11},{10,... | collective-permute-start | bytes 442376 | tf_op jit(solution)/shard_map/ppermute | solution.py:280
  14.7 9.0 %collective-permute-start.9 = (bf16[288,512]{1,0:T(8,128)(2,1)S(1)}, bf16[288,512]{1,0:T(8,128)(2,1)S(1)}, u32[]{:S(2)}, u32[]{:S(2)}) collective-permute-start(bf16[288,512]{1,0:T(8,128)(2,1)S(1)} %joined.17.refs_1_), channel_id=1, source_target_pairs={{0,16},{1,17},{2,18},{3,19},{4,20},{5,21},{6,22},{7,23},{8,9},{9,8... | collective-permute-start | bytes 884744 | tf_op jit(solution)/shard_map/ppermute | solution.py:280
  16.3 2.7 %collective-permute-start.4 = (bf16[144,512]{1,0:T(8,128)(2,1)S(1)}, bf16[144,512]{1,0:T(8,128)(2,1)S(1)}, u32[]{:S(2)}, u32[]{:S(2)}) collective-permute-start(bf16[144,512]{1,0:T(8,128)(2,1)S(1)} %joined.13), channel_id=1, source_target_pairs={{0,8},{1,9},{2,10},{3,11},{4,12},{5,13},{6,14},{7,15},{8,0},{9,1},... | collective-permute-start | bytes 442376 | tf_op jit(solution)/shard_map/ppermute | solution.py:280
  16.4 2.6 %collective-permute-start.3 = (bf16[144,512]{1,0:T(8,128)(2,1)S(1)}, bf16[144,512]{1,0:T(8,128)(2,1)S(1)}, u32[]{:S(2)}, u32[]{:S(2)}) collective-permute-start(bf16[144,512]{1,0:T(8,128)(2,1)S(1)} %joined.12), channel_id=1, source_target_pairs={{0,8},{1,9},{2,10},{3,11},{4,12},{5,13},{6,14},{7,15},{8,0},{9,1},... | collective-permute-start | bytes 442376 | tf_op jit(solution)/shard_map/ppermute | solution.py:280
  17.0 5.8 %collective-permute-start.7 = (bf16[144,512]{1,0:T(8,128)(2,1)S(1)}, bf16[144,512]{1,0:T(8,128)(2,1)S(1)}, u32[]{:S(2)}, u32[]{:S(2)}) collective-permute-start(bf16[144,512]{1,0:T(8,128)(2,1)S(1)} %joined.13), channel_id=1, source_target_pairs={{0,2},{1,3},{2,0},{3,1},{4,6},{5,7},{6,4},{7,5},{8,10},{9,11},{10,... | collective-permute-start | bytes 442376 | tf_op jit(solution)/shard_map/ppermute | solution.py:280
  18.4 5.2 %collective-permute-start.5 = (bf16[144,512]{1,0:T(8,128)(2,1)S(1)}, bf16[144,512]{1,0:T(8,128)(2,1)S(1)}, u32[]{:S(2)}, u32[]{:S(2)}) collective-permute-start(bf16[144,512]{1,0:T(8,128)(2,1)S(1)} %joined.14), channel_id=1, source_target_pairs={{0,16},{1,17},{2,18},{3,19},{4,20},{5,21},{6,22},{7,23},{8,9},{9,8... | collective-permute-start | bytes 442376 | tf_op jit(solution)/shard_map/ppermute | solution.py:280
  23.7 3.4 %collective-permute-start.10 = (bf16[576,512]{1,0:T(8,128)(2,1)S(1)}, bf16[576,512]{1,0:T(8,128)(2,1)S(1)}, u32[]{:S(2)}, u32[]{:S(2)}) collective-permute-start(bf16[576,512]{1,0:T(8,128)(2,1)S(1)} %joined.18), channel_id=1, source_target_pairs={{0,8},{1,9},{2,10},{3,11},{4,12},{5,13},{6,14},{7,15},{8,0},{9,1},... | collective-permute-start | bytes 1769480 | tf_op jit(solution)/shard_map/ppermute | solution.py:280
  23.8 9.3 %collective-permute-start.6 = (bf16[288,512]{1,0:T(8,128)(2,1)S(1)}, bf16[288,512]{1,0:T(8,128)(2,1)S(1)}, u32[]{:S(2)}, u32[]{:S(2)}) collective-permute-start(bf16[288,512]{1,0:T(8,128)(2,1)S(1)} %joined.15), channel_id=1, source_target_pairs={{0,1},{1,0},{2,3},{3,2},{4,5},{5,4},{6,7},{7,6},{8,24},{9,25},{10,... | collective-permute-start | bytes 884744 | tf_op jit(solution)/shard_map/ppermute | solution.py:280
  25.4 7.7 %collective-permute-start.8 = (bf16[144,512]{1,0:T(8,128)(2,1)S(1)}, bf16[144,512]{1,0:T(8,128)(2,1)S(1)}, u32[]{:S(2)}, u32[]{:S(2)}) collective-permute-start(bf16[144,512]{1,0:T(8,128)(2,1)S(1)} %joined.16), channel_id=1, source_target_pairs={{0,16},{1,17},{2,18},{3,19},{4,20},{5,21},{6,22},{7,23},{8,9},{9,8... | collective-permute-start | bytes 442376 | tf_op jit(solution)/shard_map/ppermute | solution.py:280
  26.5 13.4 %collective-permute-start.12 = (bf16[576,512]{1,0:T(8,128)(2,1)S(1)}, bf16[576,512]{1,0:T(8,128)(2,1)S(1)}, u32[]{:S(2)}, u32[]{:S(2)}) collective-permute-start(bf16[576,512]{1,0:T(8,128)(2,1)S(1)} %joined.20), channel_id=1, source_target_pairs={{0,1},{1,0},{2,3},{3,2},{4,5},{5,4},{6,7},{7,6},{8,24},{9,25},{10,... | collective-permute-start | bytes 1769480 | tf_op jit(solution)/shard_map/ppermute | solution.py:280
  33.1 1.9 %collective-permute-start.11 = (bf16[432,512]{1,0:T(8,128)(2,1)S(1)}, bf16[432,512]{1,0:T(8,128)(2,1)S(1)}, u32[]{:S(2)}, u32[]{:S(2)}) collective-permute-start(bf16[432,512]{1,0:T(8,128)(2,1)S(1)} %joined.19), channel_id=1, source_target_pairs={{0,8},{1,9},{2,10},{3,11},{4,12},{5,13},{6,14},{7,15},{8,0},{9,1},... | collective-permute-start | bytes 1327112 | tf_op jit(solution)/shard_map/ppermute | solution.py:280
  33.4 8.2 %collective-permute-start.14 = (bf16[288,512]{1,0:T(8,128)(2,1)S(1)}, bf16[288,512]{1,0:T(8,128)(2,1)S(1)}, u32[]{:S(2)}, u32[]{:S(2)}) collective-permute-start(bf16[288,512]{1,0:T(8,128)(2,1)S(1)} %joined.22), channel_id=1, source_target_pairs={{0,1},{1,0},{2,3},{3,2},{4,5},{5,4},{6,7},{7,6},{8,24},{9,25},{10,... | collective-permute-start | bytes 884744 | tf_op jit(solution)/shard_map/ppermute | solution.py:280
  39.9 6.5 %collective-permute-start.13 = (bf16[576,512]{1,0:T(8,128)(2,1)S(1)}, bf16[576,512]{1,0:T(8,128)(2,1)S(1)}, u32[]{:S(2)}, u32[]{:S(2)}) collective-permute-start(bf16[576,512]{1,0:T(8,128)(2,1)S(1)} %joined.21), channel_id=1, source_target_pairs={{0,8},{1,9},{2,10},{3,11},{4,12},{5,13},{6,14},{7,15},{8,0},{9,1},... | collective-permute-start | bytes 1769480 | tf_op jit(solution)/shard_map/ppermute | solution.py:280
  41.7 4.8 %collective-permute-start.15 = (bf16[288,512]{1,0:T(8,128)(2,1)S(1)}, bf16[288,512]{1,0:T(8,128)(2,1)S(1)}, u32[]{:S(2)}, u32[]{:S(2)}) collective-permute-start(bf16[288,512]{1,0:T(8,128)(2,1)S(1)} %joined.23), channel_id=1, source_target_pairs={{0,8},{1,9},{2,10},{3,11},{4,12},{5,13},{6,14},{7,15},{8,0},{9,1},... | collective-permute-start | bytes 884744 | tf_op jit(solution)/shard_map/ppermute | solution.py:280
  41.7 4.7 %copy-start = (f32[2048]{0:T(1024)S(1)}, f32[2048]{0:T(1024)}, u32[]{:S(2)}) copy-start(f32[2048]{0:T(1024)} %param.9) | copy-start | bytes 24580

commit v3 on v2

--- a/solution.py
+++ b/solution.py
@@ -105,7 +105,8 @@
     width = centres_ref.shape[1]
     alpha = math.log2(math.e) * 2.0 * scale / width
     rows, terms = pieces(shard_refs, count)
-    per = max(1, chunk // count)
+    most = max(1, chunk // count)
+    per = -(-len(rows) // -(-len(rows) // most))
     groups = [
         (jnp.concatenate(rows[i : i + per], axis=0), jnp.concatenate(terms[i : i + per], axis=1))
         for i in range(0, len(rows), per)
@@ -250,17 +251,20 @@
     return out if first or last else (*out, *state[4:])
 
 
-def joined_kernel(*refs):
+def joined_kernel(halves, *refs):
     out_ref, first = refs[-1], 0
-    for ref in refs[1:-1]:
-        out_ref[first : first + ref.shape[0], :] = ref[...]
-        first += ref.shape[0]
-
-
-def joined(parts, token):
-    rows = sum(p.shape[0] for p in parts)
+    for ref, half in zip(refs[1:-1], halves):
+        skip = ref.shape[0] // 2 if half else 0
+        rows = ref.shape[0] - skip
+        out_ref[first : first + rows, :] = ref[skip : skip + rows, :]
+        first += rows
+
+
+def joined(parts, token, halves=()):
+    half = [i in halves for i in range(len(parts))]
+    rows = sum(p.shape[0] // 2 if h else p.shape[0] for p, h in zip(parts, half))
     return pl.pallas_call(
-        joined_kernel,
+        functools.partial(joined_kernel, half),
         out_shape=pltpu.VMEM((rows, parts[0].shape[1]), BF16),
         in_specs=[VMEM] * (len(parts) + 1),
         out_specs=VMEM,
@@ -290,6 +294,12 @@
 
     def other_way(array):
         return swap(array, lambda b, g: (b ^ 2) * grp + g if b & 1 else b * grp + (g ^ 1))
+
+    def first_mix(array):
+        return swap(array, lambda b, g: b * grp + (g ^ 2 if b & 1 else g ^ 4))
+
+    def second_mix(array):
+        return swap(array, lambda b, g: b * grp + (g ^ 4 if b & 1 else g ^ 2))
 
     own = gather(table, row_ids, potentials)
     bit = grp // 2
@@ -299,25 +309,26 @@
     look = functools.partial(visit, count=count, centroids=centroids, scale=scale)
     far = grp_bit(own, 4)
     near = grp_bit(own, 2)
+    a = one_way(own)
     state = look([own, core(own)], state=None, cost=0.01)
     t = state[3]
-    a = one_way(joined([own], t))
-    near_core = core(joined([near], t))
-    two = joined([near, far], t)
+    far_on = joined([far], t)
+    both = grp_bit(far_on, 2)
+    first_core = core(joined([a, near, far], far_on))
+    two = joined([near, far], far_on)
     a_two = one_way(two)
-    both = grp_bit(joined([far], t), 2)
-    far_core = core(joined([far], t))
-    state = look([near, far, near_core, far_core], state=state)
+    b = other_way(joined([own, a], far_on))
+    state = look([a, near, far, first_core], state=state)
     t = state[3]
-    b = other_way(joined([own, a], t))
-    b_four = other_way(joined([two, a_two], t))
-    a_both = one_way(joined([both], t))
-    second_core = core(joined([a, a_two, both], t))
-    state = look([a, a_two, both, second_core], state=state)
+    both_on = joined([both], t)
+    a_both = one_way(both_on)
+    b_four = other_way(joined([two, a_two], both_on))
+    second_core = core(joined([b, a_two, both], both_on))
+    state = look([b, a_two], state=state, cost=3.0)
     t = state[3]
     b_two = other_way(joined([both, a_both], t))
-    third_core = core(joined([b, a_both], t))
-    state = look([b, a_both, third_core], state=state)
+    a_both_core = core(joined([a_both], t))
+    state = look([both, second_core, a_both, a_both_core], state=state)
     t = state[3]
     b_four_core = core(joined([b_four], t))
     b_two_core = core(joined([b_two], t))

time: 53.1 us -> 50.7 us (0.955)
  waiting for transfers between devices: 6.07 us -> 3.88 us
    ppermute x16 -> x15, waiting for transfers between devices: 6.07 us -> 3.88 us  [swap(): return lax.ppermute(array, AXES, route)]
    ppermute x16 -> x15, starting transfers between devices: 15.3 us -> 15.2 us  [swap(): return lax.ppermute(array, AXES, route)]
  transfers between devices with their start and end apart: 16 -> 15, of which waited for: 6 -> 4; matrix products, arithmetic and copies ran while one was open for 0% -> 0% of each run, Pallas kernels for 42% -> 44%
where the time goes in v3:
time: 50.7 us; the launch traced here: 50.6 us
  Pallas kernels  30.5 us (60%)
  starting transfers between devices  15.2 us (30%)
  waiting for transfers between devices  3.88 us (8%)
  between operations  0.97 us (2%)
    pallas_call x6, Pallas kernels, visit(): pl.pallas_call(functools.partial(visit_kernel, len(shards), count, block,...  28.3 us
    ppermute x15, starting transfers between devices, swap(): return lax.ppermute(array, AXES, route)  15.2 us
    ppermute x15, waiting for transfers between devices, swap(): return lax.ppermute(array, AXES, route)  3.88 us
    pallas_call x1, Pallas kernels, gather(): pl.pallas_call(gather_kernel, out_shape=pltpu.VMEM((count + EXTRA, width)...  1.94 us
  transfers between devices with their start and end apart: 15, of which 4 were waited for; matrix products, arithmetic and copies ran while one was open for 0% of the time, Pallas kernels for 44%

profile of v3, /device:TPU:0, one launch (start us, length us, event | category | flops | bytes accessed | tf_op | source)
XLA Modules:
  0.0 50.6 jit_solution(863935630447402784)
XLA Ops:
  0.6 1.9 %gather.1.refs_0_.refs_1_ = bf16[144,512]{1,0:T(8,128)(2,1)S(1)} custom-call(bf16[2048,512]{1,0:T(8,128)(2,1)} %table_ref.1, s32[1,128]{1,0:T(1,128)} %bitcast.5, bf16[1,128]{1,0:T(2,128)(2,1)} %bitcast.6), custom_call_target="tpu_custom_call" | custom-call | tf_op jit(solution)/shard_map/gather/pallas_call | solution.py:69
  2.6 0.5 %collective-permute-start = (bf16[144,512]{1,0:T(8,128)(2,1)S(1)}, bf16[144,512]{1,0:T(8,128)(2,1)S(1)}, u32[]{:S(2)}, u32[]{:S(2)}) collective-permute-start(bf16[144,512]{1,0:T(8,128)(2,1)S(1)} %gather.1.refs_0_.refs_1_), channel_id=1, source_target_pairs={{0,8},{1,9},{2,10},{3,11},{4,12},{5,13},{6,14},{7,15},{8,0},{9,1},... | collective-permute-start | bytes 442376 | tf_op jit(solution)/shard_map/ppermute | solution.py:284
  3.1 3.7 %collective-permute-start.1 = (bf16[144,512]{1,0:T(8,128)(2,1)S(1)}, bf16[144,512]{1,0:T(8,128)(2,1)S(1)}, u32[]{:S(2)}, u32[]{:S(2)}) collective-permute-start(bf16[144,512]{1,0:T(8,128)(2,1)S(1)} %gather.1.refs_0_.refs_1_), channel_id=1, source_target_pairs={{0,4},{1,5},{2,6},{3,7},{4,0},{5,1},{6,2},{7,3},{8,12},{9,13},{10,... | collective-permute-start | bytes 442376 | tf_op jit(solution)/shard_map/ppermute | solution.py:284
  6.8 1.6 %collective-permute-start.4 = (bf16[144,512]{1,0:T(8,128)(2,1)S(1)}, bf16[144,512]{1,0:T(8,128)(2,1)S(1)}, u32[]{:S(2)}, u32[]{:S(2)}) collective-permute-start(bf16[144,512]{1,0:T(8,128)(2,1)S(1)} %gather.1.refs_0_.refs_1_), channel_id=1, source_target_pairs={{0,2},{1,3},{2,0},{3,1},{4,6},{5,7},{6,4},{7,5},{8,10},{9,11},{10,... | collective-permute-start | bytes 442376 | tf_op jit(solution)/shard_map/ppermute | solution.py:284
  8.3 1.5 %collective-permute-start.3 = (bf16[144,512]{1,0:T(8,128)(2,1)S(1)}, bf16[144,512]{1,0:T(8,128)(2,1)S(1)}, u32[]{:S(2)}, u32[]{:S(2)}) collective-permute-start(bf16[144,512]{1,0:T(8,128)(2,1)S(1)} %gather.1.refs_0_.refs_1_), channel_id=1, source_target_pairs={{0,16},{1,17},{2,18},{3,19},{4,20},{5,21},{6,22},{7,23},{8,9},{9,8... | collective-permute-start | bytes 442376 | tf_op jit(solution)/shard_map/ppermute | solution.py:284
  9.8 0.0 collective-permute-done.refs_1_
  9.8 3.1 %visit.6 = (f32[2048,128]{1,0:T(8,128)S(1)}, f32[2048,128]{1,0:T(8,128)S(1)}, f32[2048,512]{1,0:T(8,128)S(1)}, f32[8,128]{1,0:T(8,128)S(1)}, f32[16,128]{1,0:T(8,128)S(1)}, /*index=5*/bf16[2048,512]{1,0:T(8,128)(2,1)S(1)}) custom-call(bf16[144,512]{1,0:T(8,128)(2,1)S(1)} %gather.1.refs_0_.refs_1_, bf16[144,512]{1,0:T(8,128)(2,1)S(1)} %collective-permute-done.refs_1_, ...), custom_call_target="tpu_custom_call" | custom-call | flops 10737418 | bytes 1024 | tf_op jit(solution)/shard_map/visit/pallas_call | solution.py:240
  12.9 1.5 %collective-permute-done.1.refs_1_.refs_3_.refs_2_ = bf16[144,512]{1,0:T(8,128)(2,1)S(1)} collective-permute-done((bf16[144,512]{1,0:T(8,128)(2,1)S(1)}, bf16[144,512]{1,0:T(8,128)(2,1)S(1)}, u32[]{:S(2)}, u32[]{:S(2)}) %collective-permute-start.1) | collective-permute-done | bytes 147488 | tf_op jit(solution)/shard_map/ppermute | solution.py:284
  14.5 0.2 collective-permute-done.4.refs_2_.refs_1_
  14.7 0.0 collective-permute-done.3.refs_1_.refs_0_.refs_2_
  14.7 0.1 collective-permute-start.5
  14.8 1.6 %collective-permute-start.7 = (bf16[288,512]{1,0:T(8,128)(2,1)S(1)}, bf16[288,512]{1,0:T(8,128)(2,1)S(1)}, u32[]{:S(2)}, u32[]{:S(2)}) collective-permute-start(bf16[288,512]{1,0:T(8,128)(2,1)S(1)} %joined.15.refs_1_), channel_id=1, source_target_pairs={{0,16},{1,17},{2,18},{3,19},{4,20},{5,21},{6,22},{7,23},{8,9},{9,8... | collective-permute-start | bytes 884744 | tf_op jit(solution)/shard_map/ppermute | solution.py:284
  16.4 1.6 %collective-permute-start.6 = (bf16[288,512]{1,0:T(8,128)(2,1)S(1)}, bf16[288,512]{1,0:T(8,128)(2,1)S(1)}, u32[]{:S(2)}, u32[]{:S(2)}) collective-permute-start(bf16[288,512]{1,0:T(8,128)(2,1)S(1)} %joined.14), channel_id=1, source_target_pairs={{0,1},{1,0},{2,3},{3,2},{4,5},{5,4},{6,7},{7,6},{8,24},{9,25},{10,... | collective-permute-start | bytes 884744 | tf_op jit(solution)/shard_map/ppermute | solution.py:284
  18.0 1.4 %collective-permute-start.2 = (bf16[144,512]{1,0:T(8,128)(2,1)S(1)}, bf16[144,512]{1,0:T(8,128)(2,1)S(1)}, u32[]{:S(2)}, u32[]{:S(2)}) collective-permute-start(bf16[144,512]{1,0:T(8,128)(2,1)S(1)} %joined.11.refs_0_), channel_id=1, source_target_pairs={{0,2},{1,3},{2,0},{3,1},{4,6},{5,7},{6,4},{7,5},{8,10},{9,11},{10,... | collective-permute-start | bytes 442376 | tf_op jit(solution)/shard_map/ppermute | solution.py:284
  19.5 0.0 collective-permute-done.5.refs_3_
  19.5 4.7 %visit.7 = (f32[2048,128]{1,0:T(8,128)S(1)}, f32[2048,128]{1,0:T(8,128)S(1)}, f32[2048,512]{1,0:T(8,128)S(1)}, f32[8,128]{1,0:T(8,128)S(1)}) custom-call(bf16[144,512]{1,0:T(8,128)(2,1)S(1)} %collective-permute-done.3.refs_1_.refs_0_.refs_2_, ...), custom_call_target="tpu_custom_call", output_to_operand_aliasing={{0}: (5, {}), {1}: (6, {}), {2}: (7, {})} | custom-call | flops 1288490240 | bytes 1024 | tf_op jit(solution)/shard_map/visit/pallas_call | solution.py:240
  24.2 0.0 collective-permute-done.2.refs_1_.refs_3_.refs_0_
  24.3 0.6 %collective-permute-start.9 = (bf16[144,512]{1,0:T(8,128)(2,1)S(1)}, bf16[144,512]{1,0:T(8,128)(2,1)S(1)}, u32[]{:S(2)}, u32[]{:S(2)}) collective-permute-start(bf16[144,512]{1,0:T(8,128)(2,1)S(1)} %joined.13.refs_0_), channel_id=1, source_target_pairs={{0,16},{1,17},{2,18},{3,19},{4,20},{5,21},{6,22},{7,23},{8,9},{9,8... | collective-permute-start | bytes 442376 | tf_op jit(solution)/shard_map/ppermute | solution.py:284
  24.8 0.0 collective-permute-done.7.refs_2_.refs_1_
  24.9 1.3 %collective-permute-start.11 = (bf16[576,512]{1,0:T(8,128)(2,1)S(1)}, bf16[576,512]{1,0:T(8,128)(2,1)S(1)}, u32[]{:S(2)}, u32[]{:S(2)}) collective-permute-start(bf16[576,512]{1,0:T(8,128)(2,1)S(1)} %joined.18), channel_id=1, source_target_pairs={{0,1},{1,0},{2,3},{3,2},{4,5},{5,4},{6,7},{7,6},{8,24},{9,25},{10,... | collective-permute-start | bytes 1769480 | tf_op jit(solution)/shard_map/ppermute | solution.py:284
  26.2 0.0 collective-permute-done.6.refs_1_.refs_0_
  26.3 0.1 collective-permute-start.8
  26.4 3.4 %visit.8 = (f32[2048,128]{1,0:T(8,128)S(1)}, f32[2048,128]{1,0:T(8,128)S(1)}, f32[2048,512]{1,0:T(8,128)S(1)}, f32[8,128]{1,0:T(8,128)S(1)}) custom-call(bf16[288,512]{1,0:T(8,128)(2,1)S(1)} %collective-permute-done.6.refs_1_.refs_0_, ...), custom_call_target="tpu_custom_call", output_to_operand_aliasing={{0}: (3, {}), {1}: (4, {}), {2}: (5, {})} | custom-call | flops 6442450944 | bytes 1024 | tf_op jit(solution)/shard_map/visit/pallas_call | solution.py:240
  29.7 1.3 %collective-permute-done.9.refs_1_.refs_2_ = bf16[144,512]{1,0:T(8,128)(2,1)S(1)} collective-permute-done((bf16[144,512]{1,0:T(8,128)(2,1)S(1)}, bf16[144,512]{1,0:T(8,128)(2,1)S(1)}, u32[]{:S(2)}, u32[]{:S(2)}) %collective-permute-start.9) | collective-permute-done | bytes 147488 | tf_op jit(solution)/shard_map/ppermute | solution.py:284
  31.1 0.1 collective-permute-start.10
  31.2 0.5 %collective-permute-start.13 = (bf16[288,512]{1,0:T(8,128)(2,1)S(1)}, bf16[288,512]{1,0:T(8,128)(2,1)S(1)}, u32[]{:S(2)}, u32[]{:S(2)}) collective-permute-start(bf16[288,512]{1,0:T(8,128)(2,1)S(1)} %joined.20), channel_id=1, source_target_pairs={{0,1},{1,0},{2,3},{3,2},{4,5},{5,4},{6,7},{7,6},{8,24},{9,25},{10,... | collective-permute-start | bytes 884744 | tf_op jit(solution)/shard_map/ppermute | solution.py:284
  31.7 0.8 %collective-permute-done.10.refs_3_ = bf16[144,512]{1,0:T(8,128)(2,1)S(1)} collective-permute-done((bf16[144,512]{1,0:T(8,128)(2,1)S(1)}, bf16[144,512]{1,0:T(8,128)(2,1)S(1)}, u32[]{:S(2)}, u32[]{:S(2)}) %collective-permute-start.10) | collective-permute-done | bytes 147488 | tf_op jit(solution)/shard_map/ppermute | solution.py:284
  32.5 0.0 collective-permute-done.8.refs_1_
  32.5 6.1 %visit.9 = (f32[2048,128]{1,0:T(8,128)S(1)}, f32[2048,128]{1,0:T(8,128)S(1)}, f32[2048,512]{1,0:T(8,128)S(1)}, f32[8,128]{1,0:T(8,128)S(1)}) custom-call(bf16[144,512]{1,0:T(8,128)(2,1)S(1)} %collective-permute-done.2.refs_1_.refs_3_.refs_0_, ...), custom_call_target="tpu_custom_call", output_to_operand_aliasing={{0}: (5, {}), {1}: (6, {}), {2}: (7, {})} | custom-call | flops 1717986944 | bytes 1024 | tf_op jit(solution)/shard_map/visit/pallas_call | solution.py:240
  38.6 0.0 collective-permute-done.11.refs_1_.refs_0_
  38.7 0.2 collective-permute-start.12
  38.9 0.0 collective-permute-done.13.refs_1_
  38.9 0.4 collective-permute-start.14
  39.3 0.0 copy-start
  39.4 4.8 %visit.10 = (f32[2048,128]{1,0:T(8,128)S(1)}, f32[2048,128]{1,0:T(8,128)S(1)}, f32[2048,512]{1,0:T(8,128)S(1)}, f32[8,128]{1,0:T(8,128)}) custom-call(bf16[576,512]{1,0:T(8,128)(2,1)S(1)} %collective-permute-done.11.refs_1_.refs_0_, bf16[288,512]{1,0:T(8,128)(2,1)S(1)} %collective-permute-done.13.refs_1_, ...), custom_call_target="tpu_custom_call", output_to_operand_aliasing={{0}: (3, {}), {1}: (4, {}), {2}: (5, {})} | custom-call | flops 1288490240 | bytes 1024 | tf_op jit(solution)/shard_map/visit/pallas_call | solution.py:240
  44.1 0.0 collective-permute-done.14.refs_1_
  44.2 0.0 collective-permute-done.12.refs_0_
  44.2 0.0 copy-done
  44.2 6.2 %visit.11 = (f32[2048,512]{1,0:T(8,128)}, f32[16,128]{1,0:T(8,128)}) custom-call(bf16[576,512]{1,0:T(8,128)(2,1)S(1)} %collective-permute-done.12.refs_0_, bf16[288,512]{1,0:T(8,128)(2,1)S(1)} %collective-permute-done.14.refs_1_, bf16[2048,512]{1,0:T(8,128)(2,1)S(1)} %get-tuple-element.26.refs_4_.refs_2_, f32[2048,128]{1,0:T(8,128)S(1)} %get-tuple-element.42.refs_3_, ...), custom_call_target="tpu_custom_call" | custom-call | flops 1288490240 | bytes 1024 | tf_op jit(solution)/shard_map/visit/pallas_call | solution.py:240
  (11 shorter events, 0.3 us)
Async XLA Ops:
  2.6 7.3 %collective-permute-start = (bf16[144,512]{1,0:T(8,128)(2,1)S(1)}, bf16[144,512]{1,0:T(8,128)(2,1)S(1)}, u32[]{:S(2)}, u32[]{:S(2)}) collective-permute-start(bf16[144,512]{1,0:T(8,128)(2,1)S(1)} %gather.1.refs_0_.refs_1_), channel_id=1, source_target_pairs={{0,8},{1,9},{2,10},{3,11},{4,12},{5,13},{6,14},{7,15},{8,0},{9,1},... | collective-permute-start | bytes 442376 | tf_op jit(solution)/shard_map/ppermute | solution.py:284
  3.1 11.4 %collective-permute-start.1 = (bf16[144,512]{1,0:T(8,128)(2,1)S(1)}, bf16[144,512]{1,0:T(8,128)(2,1)S(1)}, u32[]{:S(2)}, u32[]{:S(2)}) collective-permute-start(bf16[144,512]{1,0:T(8,128)(2,1)S(1)} %gather.1.refs_0_.refs_1_), channel_id=1, source_target_pairs={{0,4},{1,5},{2,6},{3,7},{4,0},{5,1},{6,2},{7,3},{8,12},{9,13},{10,... | collective-permute-start | bytes 442376 | tf_op jit(solution)/shard_map/ppermute | solution.py:284
  6.8 7.9 %collective-permute-start.4 = (bf16[144,512]{1,0:T(8,128)(2,1)S(1)}, bf16[144,512]{1,0:T(8,128)(2,1)S(1)}, u32[]{:S(2)}, u32[]{:S(2)}) collective-permute-start(bf16[144,512]{1,0:T(8,128)(2,1)S(1)} %gather.1.refs_0_.refs_1_), channel_id=1, source_target_pairs={{0,2},{1,3},{2,0},{3,1},{4,6},{5,7},{6,4},{7,5},{8,10},{9,11},{10,... | collective-permute-start | bytes 442376 | tf_op jit(solution)/shard_map/ppermute | solution.py:284
  8.3 6.3 %collective-permute-start.3 = (bf16[144,512]{1,0:T(8,128)(2,1)S(1)}, bf16[144,512]{1,0:T(8,128)(2,1)S(1)}, u32[]{:S(2)}, u32[]{:S(2)}) collective-permute-start(bf16[144,512]{1,0:T(8,128)(2,1)S(1)} %gather.1.refs_0_.refs_1_), channel_id=1, source_target_pairs={{0,16},{1,17},{2,18},{3,19},{4,20},{5,21},{6,22},{7,23},{8,9},{9,8... | collective-permute-start | bytes 442376 | tf_op jit(solution)/shard_map/ppermute | solution.py:284
  14.7 4.8 %collective-permute-start.5 = (bf16[432,512]{1,0:T(8,128)(2,1)S(1)}, bf16[432,512]{1,0:T(8,128)(2,1)S(1)}, u32[]{:S(2)}, u32[]{:S(2)}) collective-permute-start(bf16[432,512]{1,0:T(8,128)(2,1)S(1)} %joined.12), channel_id=1, source_target_pairs={{0,8},{1,9},{2,10},{3,11},{4,12},{5,13},{6,14},{7,15},{8,0},{9,1},... | collective-permute-start | bytes 1327112 | tf_op jit(solution)/shard_map/ppermute | solution.py:284
  14.8 10.0 %collective-permute-start.7 = (bf16[288,512]{1,0:T(8,128)(2,1)S(1)}, bf16[288,512]{1,0:T(8,128)(2,1)S(1)}, u32[]{:S(2)}, u32[]{:S(2)}) collective-permute-start(bf16[288,512]{1,0:T(8,128)(2,1)S(1)} %joined.15.refs_1_), channel_id=1, source_target_pairs={{0,16},{1,17},{2,18},{3,19},{4,20},{5,21},{6,22},{7,23},{8,9},{9,8... | collective-permute-start | bytes 884744 | tf_op jit(solution)/shard_map/ppermute | solution.py:284
  16.4 9.8 %collective-permute-start.6 = (bf16[288,512]{1,0:T(8,128)(2,1)S(1)}, bf16[288,512]{1,0:T(8,128)(2,1)S(1)}, u32[]{:S(2)}, u32[]{:S(2)}) collective-permute-start(bf16[288,512]{1,0:T(8,128)(2,1)S(1)} %joined.14), channel_id=1, source_target_pairs={{0,1},{1,0},{2,3},{3,2},{4,5},{5,4},{6,7},{7,6},{8,24},{9,25},{10,... | collective-permute-start | bytes 884744 | tf_op jit(solution)/shard_map/ppermute | solution.py:284
  18.0 6.2 %collective-permute-start.2 = (bf16[144,512]{1,0:T(8,128)(2,1)S(1)}, bf16[144,512]{1,0:T(8,128)(2,1)S(1)}, u32[]{:S(2)}, u32[]{:S(2)}) collective-permute-start(bf16[144,512]{1,0:T(8,128)(2,1)S(1)} %joined.11.refs_0_), channel_id=1, source_target_pairs={{0,2},{1,3},{2,0},{3,1},{4,6},{5,7},{6,4},{7,5},{8,10},{9,11},{10,... | collective-permute-start | bytes 442376 | tf_op jit(solution)/shard_map/ppermute | solution.py:284
  24.3 6.8 %collective-permute-start.9 = (bf16[144,512]{1,0:T(8,128)(2,1)S(1)}, bf16[144,512]{1,0:T(8,128)(2,1)S(1)}, u32[]{:S(2)}, u32[]{:S(2)}) collective-permute-start(bf16[144,512]{1,0:T(8,128)(2,1)S(1)} %joined.13.refs_0_), channel_id=1, source_target_pairs={{0,16},{1,17},{2,18},{3,19},{4,20},{5,21},{6,22},{7,23},{8,9},{9,8... | collective-permute-start | bytes 442376 | tf_op jit(solution)/shard_map/ppermute | solution.py:284
  24.9 13.7 %collective-permute-start.11 = (bf16[576,512]{1,0:T(8,128)(2,1)S(1)}, bf16[576,512]{1,0:T(8,128)(2,1)S(1)}, u32[]{:S(2)}, u32[]{:S(2)}) collective-permute-start(bf16[576,512]{1,0:T(8,128)(2,1)S(1)} %joined.18), channel_id=1, source_target_pairs={{0,1},{1,0},{2,3},{3,2},{4,5},{5,4},{6,7},{7,6},{8,24},{9,25},{10,... | collective-permute-start | bytes 1769480 | tf_op jit(solution)/shard_map/ppermute | solution.py:284
  26.3 6.2 %collective-permute-start.8 = (bf16[720,512]{1,0:T(8,128)(2,1)S(1)}, bf16[720,512]{1,0:T(8,128)(2,1)S(1)}, u32[]{:S(2)}, u32[]{:S(2)}) collective-permute-start(bf16[720,512]{1,0:T(8,128)(2,1)S(1)} %joined.16), channel_id=1, source_target_pairs={{0,8},{1,9},{2,10},{3,11},{4,12},{5,13},{6,14},{7,15},{8,0},{9,1},... | collective-permute-start | bytes 2211848 | tf_op jit(solution)/shard_map/ppermute | solution.py:284
  31.1 1.4 %collective-permute-start.10 = (bf16[144,512]{1,0:T(8,128)(2,1)S(1)}, bf16[144,512]{1,0:T(8,128)(2,1)S(1)}, u32[]{:S(2)}, u32[]{:S(2)}) collective-permute-start(bf16[144,512]{1,0:T(8,128)(2,1)S(1)} %joined.17), channel_id=1, source_target_pairs={{0,8},{1,9},{2,10},{3,11},{4,12},{5,13},{6,14},{7,15},{8,0},{9,1},... | collective-permute-start | bytes 442376 | tf_op jit(solution)/shard_map/ppermute | solution.py:284
  31.2 7.7 %collective-permute-start.13 = (bf16[288,512]{1,0:T(8,128)(2,1)S(1)}, bf16[288,512]{1,0:T(8,128)(2,1)S(1)}, u32[]{:S(2)}, u32[]{:S(2)}) collective-permute-start(bf16[288,512]{1,0:T(8,128)(2,1)S(1)} %joined.20), channel_id=1, source_target_pairs={{0,1},{1,0},{2,3},{3,2},{4,5},{5,4},{6,7},{7,6},{8,24},{9,25},{10,... | collective-permute-start | bytes 884744 | tf_op jit(solution)/shard_map/ppermute | solution.py:284
  38.7 5.5 %collective-permute-start.12 = (bf16[576,512]{1,0:T(8,128)(2,1)S(1)}, bf16[576,512]{1,0:T(8,128)(2,1)S(1)}, u32[]{:S(2)}, u32[]{:S(2)}) collective-permute-start(bf16[576,512]{1,0:T(8,128)(2,1)S(1)} %joined.19), channel_id=1, source_target_pairs={{0,8},{1,9},{2,10},{3,11},{4,12},{5,13},{6,14},{7,15},{8,0},{9,1},... | collective-permute-start | bytes 1769480 | tf_op jit(solution)/shard_map/ppermute | solution.py:284
  38.9 5.2 %collective-permute-start.14 = (bf16[288,512]{1,0:T(8,128)(2,1)S(1)}, bf16[288,512]{1,0:T(8,128)(2,1)S(1)}, u32[]{:S(2)}, u32[]{:S(2)}) collective-permute-start(bf16[288,512]{1,0:T(8,128)(2,1)S(1)} %joined.21), channel_id=1, source_target_pairs={{0,8},{1,9},{2,10},{3,11},{4,12},{5,13},{6,14},{7,15},{8,0},{9,1},... | collective-permute-start | bytes 884744 | tf_op jit(solution)/shard_map/ppermute | solution.py:284
  39.3 4.8 %copy-start = (f32[2048]{0:T(1024)S(1)}, f32[2048]{0:T(1024)}, u32[]{:S(2)}) copy-start(f32[2048]{0:T(1024)} %param.9) | copy-start | bytes 24580

commit v4 on v3

--- a/solution.py
+++ b/solution.py
@@ -12,6 +12,7 @@
 AXES = ("blk", "grp")
 EXTRA = 16
 LANES = 128
+OUT = 256
 VMEM = pl.BlockSpec(memory_space=pltpu.VMEM)
 NT = (((1,), (1,)), ((), ()))
 
@@ -170,19 +171,22 @@
                     refs[3][...] = top[0:8, :]
                 refs[0][at, :] = top
                 refs[1][at, :] = mass
-        for f in range(0, width, LANES):
-            lane = slice(f, f + LANES)
-            value = numer[:, lane]
-            if acc_in is not None:
-                value = acc_in[at, lane] * shrink + value
+        step = min(OUT, block) if done and last else block
+        for r in range(0, block, step):
+            here, rows_at = slice(r, r + step), slice(j * block + r, j * block + r + step)
+            for f in range(0, width, LANES):
+                lane = slice(f, f + LANES)
+                value = numer[here, lane]
+                if acc_in is not None:
+                    value = acc_in[rows_at, lane] * shrink[here] + value
+                if done and last:
+                    value = value * inverse[here]
+                acc_ref[rows_at, lane] = value
             if done and last:
-                value = value * inverse
-            acc_ref[at, lane] = value
-        if done and last:
-            out_copy(j).start()
+                out_copy((j * block + r) // step).start()
 
     def out_copy(j):
-        at = pl.ds(j * block, block)
+        at = pl.ds(j * min(OUT, block), min(OUT, block))
         return pltpu.make_async_copy(held_ref.at[at, :], means_ref.at[at, :], sems.at[j])
 
     def load(j):
@@ -205,7 +209,7 @@
             ahead = scores(units[i + 1])
         weigh(u, *soft(u, now))
     if last:
-        for j in range(total // block):
+        for j in range(total // min(OUT, block)):
             out_copy(j).wait()
 
 
@@ -219,7 +223,7 @@
     if last:
         out_shape = [jax.ShapeDtypeStruct((total, width), F32), jax.ShapeDtypeStruct(lines, F32)]
         out_specs = [pl.BlockSpec(memory_space=pltpu.HBM), VMEM]
-        scratch = [pltpu.VMEM((total, width), F32), pltpu.SemaphoreType.DMA((total // block,))]
+        scratch = [pltpu.VMEM((total, width), F32), pltpu.SemaphoreType.DMA((total // min(OUT, block),))]
     else:
         shapes = [(total, LANES), (total, LANES), (total, width), (8, LANES)] + ([lines] if first else [])
         out_shape = [pltpu.VMEM(shape, F32) for shape in shapes]
@@ -317,8 +321,8 @@
     first_core = core(joined([a, near, far], far_on))
     two = joined([near, far], far_on)
     a_two = one_way(two)
-    b = other_way(joined([own, a], far_on))
-    state = look([a, near, far, first_core], state=state)
+    b = other_way(joined([own, a], two))
+    state = look([a, near, far, first_core], state=state, cost=0.1)
     t = state[3]
     both_on = joined([both], t)
     a_both = one_way(both_on)
@@ -328,12 +332,12 @@
     t = state[3]
     b_two = other_way(joined([both, a_both], t))
     a_both_core = core(joined([a_both], t))
-    state = look([both, second_core, a_both, a_both_core], state=state)
+    state = look([both, second_core, a_both, a_both_core], state=state, cost=0.4)
     t = state[3]
     b_four_core = core(joined([b_four], t))
     b_two_core = core(joined([b_two], t))
-    state = look([b_four, b_two], state=state)
-    means, potential = look([b_four_core, b_two_core], state=state, balance=balance)
+    state = look([b_four, b_two], state=state, cost=1.0)
+    means, potential = look([b_four_core, b_two_core], state=state, balance=balance, cost=1.0)
     return means, potential.reshape(balance.shape)
 
 

time: 50.7 us -> 50.4 us (level)
  no operation moved by 1% of the time
where the time goes in v4:
time: 50.4 us; the launch traced here: 50.2 us
  Pallas kernels  30.2 us (60%)
  starting transfers between devices  15.2 us (30%)
  waiting for transfers between devices  3.83 us (8%)
  between operations  0.97 us (2%)
    pallas_call x6, Pallas kernels, visit(): pl.pallas_call(functools.partial(visit_kernel, len(shards), count, block,...  28 us
    ppermute x15, starting transfers between devices, swap(): return lax.ppermute(array, AXES, route)  15.2 us
    ppermute x15, waiting for transfers between devices, swap(): return lax.ppermute(array, AXES, route)  3.83 us
    pallas_call x1, Pallas kernels, gather(): pl.pallas_call(gather_kernel, out_shape=pltpu.VMEM((count + EXTRA, width)...  1.94 us
  transfers between devices with their start and end apart: 15, of which 4 were waited for; matrix products, arithmetic and copies ran while one was open for 0% of the time, Pallas kernels for 44%

profile of v4, /device:TPU:0, one launch (start us, length us, event | category | flops | bytes accessed | tf_op | source)
XLA Modules:
  0.0 50.2 jit_solution(14520809567843537859)
XLA Ops:
  0.6 1.9 %gather.1.refs_0_.refs_1_ = bf16[144,512]{1,0:T(8,128)(2,1)S(1)} custom-call(bf16[2048,512]{1,0:T(8,128)(2,1)} %table_ref.1, s32[1,128]{1,0:T(1,128)} %bitcast.5, bf16[1,128]{1,0:T(2,128)(2,1)} %bitcast.6), custom_call_target="tpu_custom_call" | custom-call | tf_op jit(solution)/shard_map/gather/pallas_call | solution.py:70
  2.6 0.5 %collective-permute-start = (bf16[144,512]{1,0:T(8,128)(2,1)S(1)}, bf16[144,512]{1,0:T(8,128)(2,1)S(1)}, u32[]{:S(2)}, u32[]{:S(2)}) collective-permute-start(bf16[144,512]{1,0:T(8,128)(2,1)S(1)} %gather.1.refs_0_.refs_1_), channel_id=1, source_target_pairs={{0,8},{1,9},{2,10},{3,11},{4,12},{5,13},{6,14},{7,15},{8,0},{9,1},... | collective-permute-start | bytes 442376 | tf_op jit(solution)/shard_map/ppermute | solution.py:288
  3.1 3.7 %collective-permute-start.1 = (bf16[144,512]{1,0:T(8,128)(2,1)S(1)}, bf16[144,512]{1,0:T(8,128)(2,1)S(1)}, u32[]{:S(2)}, u32[]{:S(2)}) collective-permute-start(bf16[144,512]{1,0:T(8,128)(2,1)S(1)} %gather.1.refs_0_.refs_1_), channel_id=1, source_target_pairs={{0,4},{1,5},{2,6},{3,7},{4,0},{5,1},{6,2},{7,3},{8,12},{9,13},{10,... | collective-permute-start | bytes 442376 | tf_op jit(solution)/shard_map/ppermute | solution.py:288
  6.8 1.6 %collective-permute-start.4 = (bf16[144,512]{1,0:T(8,128)(2,1)S(1)}, bf16[144,512]{1,0:T(8,128)(2,1)S(1)}, u32[]{:S(2)}, u32[]{:S(2)}) collective-permute-start(bf16[144,512]{1,0:T(8,128)(2,1)S(1)} %gather.1.refs_0_.refs_1_), channel_id=1, source_target_pairs={{0,2},{1,3},{2,0},{3,1},{4,6},{5,7},{6,4},{7,5},{8,10},{9,11},{10,... | collective-permute-start | bytes 442376 | tf_op jit(solution)/shard_map/ppermute | solution.py:288
  8.3 1.5 %collective-permute-start.3 = (bf16[144,512]{1,0:T(8,128)(2,1)S(1)}, bf16[144,512]{1,0:T(8,128)(2,1)S(1)}, u32[]{:S(2)}, u32[]{:S(2)}) collective-permute-start(bf16[144,512]{1,0:T(8,128)(2,1)S(1)} %gather.1.refs_0_.refs_1_), channel_id=1, source_target_pairs={{0,16},{1,17},{2,18},{3,19},{4,20},{5,21},{6,22},{7,23},{8,9},{9,8... | collective-permute-start | bytes 442376 | tf_op jit(solution)/shard_map/ppermute | solution.py:288
  9.8 0.0 collective-permute-done.refs_1_
  9.8 3.1 %visit.6 = (f32[2048,128]{1,0:T(8,128)S(1)}, f32[2048,128]{1,0:T(8,128)S(1)}, f32[2048,512]{1,0:T(8,128)S(1)}, f32[8,128]{1,0:T(8,128)S(1)}, f32[16,128]{1,0:T(8,128)S(1)}, /*index=5*/bf16[2048,512]{1,0:T(8,128)(2,1)S(1)}) custom-call(bf16[144,512]{1,0:T(8,128)(2,1)S(1)} %gather.1.refs_0_.refs_1_, bf16[144,512]{1,0:T(8,128)(2,1)S(1)} %collective-permute-done.refs_1_, ...), custom_call_target="tpu_custom_call" | custom-call | flops 10737418 | bytes 1024 | tf_op jit(solution)/shard_map/visit/pallas_call | solution.py:244
  12.9 1.5 %collective-permute-done.1.refs_1_.refs_3_.refs_2_ = bf16[144,512]{1,0:T(8,128)(2,1)S(1)} collective-permute-done((bf16[144,512]{1,0:T(8,128)(2,1)S(1)}, bf16[144,512]{1,0:T(8,128)(2,1)S(1)}, u32[]{:S(2)}, u32[]{:S(2)}) %collective-permute-start.1) | collective-permute-done | bytes 147488 | tf_op jit(solution)/shard_map/ppermute | solution.py:288
  14.5 0.2 collective-permute-done.4.refs_2_.refs_1_
  14.7 0.0 collective-permute-done.3.refs_1_.refs_0_.refs_2_
  14.7 0.1 collective-permute-start.5
  14.8 1.6 %collective-permute-start.7 = (bf16[288,512]{1,0:T(8,128)(2,1)S(1)}, bf16[288,512]{1,0:T(8,128)(2,1)S(1)}, u32[]{:S(2)}, u32[]{:S(2)}) collective-permute-start(bf16[288,512]{1,0:T(8,128)(2,1)S(1)} %joined.14.refs_0_.refs_1_), channel_id=1, source_target_pairs={{0,16},{1,17},{2,18},{3,19},{4,20},{5,21},{6,22},{7,23},{8,9},{9,8... | collective-permute-start | bytes 884744 | tf_op jit(solution)/shard_map/ppermute | solution.py:288
  16.4 1.6 %collective-permute-start.6 = (bf16[288,512]{1,0:T(8,128)(2,1)S(1)}, bf16[288,512]{1,0:T(8,128)(2,1)S(1)}, u32[]{:S(2)}, u32[]{:S(2)}) collective-permute-start(bf16[288,512]{1,0:T(8,128)(2,1)S(1)} %joined.15), channel_id=1, source_target_pairs={{0,1},{1,0},{2,3},{3,2},{4,5},{5,4},{6,7},{7,6},{8,24},{9,25},{10,... | collective-permute-start | bytes 884744 | tf_op jit(solution)/shard_map/ppermute | solution.py:288
  18.0 1.4 %collective-permute-start.2 = (bf16[144,512]{1,0:T(8,128)(2,1)S(1)}, bf16[144,512]{1,0:T(8,128)(2,1)S(1)}, u32[]{:S(2)}, u32[]{:S(2)}) collective-permute-start(bf16[144,512]{1,0:T(8,128)(2,1)S(1)} %joined.11.refs_0_), channel_id=1, source_target_pairs={{0,2},{1,3},{2,0},{3,1},{4,6},{5,7},{6,4},{7,5},{8,10},{9,11},{10,... | collective-permute-start | bytes 442376 | tf_op jit(solution)/shard_map/ppermute | solution.py:288
  19.5 0.0 collective-permute-done.5.refs_3_
  19.5 4.7 %visit.7 = (f32[2048,128]{1,0:T(8,128)S(1)}, f32[2048,128]{1,0:T(8,128)S(1)}, f32[2048,512]{1,0:T(8,128)S(1)}, f32[8,128]{1,0:T(8,128)S(1)}) custom-call(bf16[144,512]{1,0:T(8,128)(2,1)S(1)} %collective-permute-done.3.refs_1_.refs_0_.refs_2_, ...), custom_call_target="tpu_custom_call", output_to_operand_aliasing={{0}: (5, {}), {1}: (6, {}), {2}: (7, {})} | custom-call | flops 322122560 | bytes 1024 | tf_op jit(solution)/shard_map/visit/pallas_call | solution.py:244
  24.2 0.0 collective-permute-done.2.refs_1_.refs_3_.refs_0_
  24.3 0.6 %collective-permute-start.9 = (bf16[144,512]{1,0:T(8,128)(2,1)S(1)}, bf16[144,512]{1,0:T(8,128)(2,1)S(1)}, u32[]{:S(2)}, u32[]{:S(2)}) collective-permute-start(bf16[144,512]{1,0:T(8,128)(2,1)S(1)} %joined.13.refs_0_), channel_id=1, source_target_pairs={{0,16},{1,17},{2,18},{3,19},{4,20},{5,21},{6,22},{7,23},{8,9},{9,8... | collective-permute-start | bytes 442376 | tf_op jit(solution)/shard_map/ppermute | solution.py:288
  24.9 0.0 collective-permute-done.7.refs_2_.refs_1_
  24.9 1.3 %collective-permute-start.11 = (bf16[576,512]{1,0:T(8,128)(2,1)S(1)}, bf16[576,512]{1,0:T(8,128)(2,1)S(1)}, u32[]{:S(2)}, u32[]{:S(2)}) collective-permute-start(bf16[576,512]{1,0:T(8,128)(2,1)S(1)} %joined.18), channel_id=1, source_target_pairs={{0,1},{1,0},{2,3},{3,2},{4,5},{5,4},{6,7},{7,6},{8,24},{9,25},{10,... | collective-permute-start | bytes 1769480 | tf_op jit(solution)/shard_map/ppermute | solution.py:288
  26.2 0.0 collective-permute-done.6.refs_1_.refs_0_
  26.3 0.1 collective-permute-start.8
  26.4 3.4 %visit.8 = (f32[2048,128]{1,0:T(8,128)S(1)}, f32[2048,128]{1,0:T(8,128)S(1)}, f32[2048,512]{1,0:T(8,128)S(1)}, f32[8,128]{1,0:T(8,128)S(1)}) custom-call(bf16[288,512]{1,0:T(8,128)(2,1)S(1)} %collective-permute-done.6.refs_1_.refs_0_, ...), custom_call_target="tpu_custom_call", output_to_operand_aliasing={{0}: (3, {}), {1}: (4, {}), {2}: (5, {})} | custom-call | flops 6442450944 | bytes 1024 | tf_op jit(solution)/shard_map/visit/pallas_call | solution.py:244
  29.7 1.3 %collective-permute-done.9.refs_1_.refs_2_ = bf16[144,512]{1,0:T(8,128)(2,1)S(1)} collective-permute-done((bf16[144,512]{1,0:T(8,128)(2,1)S(1)}, bf16[144,512]{1,0:T(8,128)(2,1)S(1)}, u32[]{:S(2)}, u32[]{:S(2)}) %collective-permute-start.9) | collective-permute-done | bytes 147488 | tf_op jit(solution)/shard_map/ppermute | solution.py:288
  31.1 0.1 collective-permute-start.10
  31.2 0.6 %collective-permute-start.13 = (bf16[288,512]{1,0:T(8,128)(2,1)S(1)}, bf16[288,512]{1,0:T(8,128)(2,1)S(1)}, u32[]{:S(2)}, u32[]{:S(2)}) collective-permute-start(bf16[288,512]{1,0:T(8,128)(2,1)S(1)} %joined.20), channel_id=1, source_target_pairs={{0,1},{1,0},{2,3},{3,2},{4,5},{5,4},{6,7},{7,6},{8,24},{9,25},{10,... | collective-permute-start | bytes 884744 | tf_op jit(solution)/shard_map/ppermute | solution.py:288
  31.7 0.8 %collective-permute-done.10.refs_3_ = bf16[144,512]{1,0:T(8,128)(2,1)S(1)} collective-permute-done((bf16[144,512]{1,0:T(8,128)(2,1)S(1)}, bf16[144,512]{1,0:T(8,128)(2,1)S(1)}, u32[]{:S(2)}, u32[]{:S(2)}) %collective-permute-start.10) | collective-permute-done | bytes 147488 | tf_op jit(solution)/shard_map/ppermute | solution.py:288
  32.5 0.0 collective-permute-done.8.refs_1_
  32.5 6.1 %visit.9 = (f32[2048,128]{1,0:T(8,128)S(1)}, f32[2048,128]{1,0:T(8,128)S(1)}, f32[2048,512]{1,0:T(8,128)S(1)}, f32[8,128]{1,0:T(8,128)S(1)}) custom-call(bf16[144,512]{1,0:T(8,128)(2,1)S(1)} %collective-permute-done.2.refs_1_.refs_3_.refs_0_, ...), custom_call_target="tpu_custom_call", output_to_operand_aliasing={{0}: (5, {}), {1}: (6, {}), {2}: (7, {})} | custom-call | flops 1717986944 | bytes 1024 | tf_op jit(solution)/shard_map/visit/pallas_call | solution.py:244
  38.6 0.0 collective-permute-done.11.refs_1_.refs_0_
  38.7 0.2 collective-permute-start.12
  38.9 0.0 collective-permute-done.13.refs_1_
  38.9 0.4 collective-permute-start.14
  39.4 0.0 copy-start
  39.4 4.6 %visit.10 = (f32[2048,128]{1,0:T(8,128)S(1)}, f32[2048,128]{1,0:T(8,128)S(1)}, f32[2048,512]{1,0:T(8,128)S(1)}, f32[8,128]{1,0:T(8,128)}) custom-call(bf16[576,512]{1,0:T(8,128)(2,1)S(1)} %collective-permute-done.11.refs_1_.refs_0_, bf16[288,512]{1,0:T(8,128)(2,1)S(1)} %collective-permute-done.13.refs_1_, ...), custom_call_target="tpu_custom_call", output_to_operand_aliasing={{0}: (3, {}), {1}: (4, {}), {2}: (5, {})} | custom-call | flops 3221225472 | bytes 1024 | tf_op jit(solution)/shard_map/visit/pallas_call | solution.py:244
  44.0 0.0 collective-permute-done.14.refs_1_
  44.0 0.0 collective-permute-done.12.refs_0_
  44.0 0.0 copy-done
  44.1 6.0 %visit.11 = (f32[2048,512]{1,0:T(8,128)}, f32[16,128]{1,0:T(8,128)}) custom-call(bf16[576,512]{1,0:T(8,128)(2,1)S(1)} %collective-permute-done.12.refs_0_, bf16[288,512]{1,0:T(8,128)(2,1)S(1)} %collective-permute-done.14.refs_1_, bf16[2048,512]{1,0:T(8,128)(2,1)S(1)} %get-tuple-element.26.refs_4_.refs_2_, f32[2048,128]{1,0:T(8,128)S(1)} %get-tuple-element.42.refs_3_, ...), custom_call_target="tpu_custom_call" | custom-call | flops 3221225472 | bytes 1024 | tf_op jit(solution)/shard_map/visit/pallas_call | solution.py:244
  (11 shorter events, 0.3 us)
Async XLA Ops:
  2.6 7.3 %collective-permute-start = (bf16[144,512]{1,0:T(8,128)(2,1)S(1)}, bf16[144,512]{1,0:T(8,128)(2,1)S(1)}, u32[]{:S(2)}, u32[]{:S(2)}) collective-permute-start(bf16[144,512]{1,0:T(8,128)(2,1)S(1)} %gather.1.refs_0_.refs_1_), channel_id=1, source_target_pairs={{0,8},{1,9},{2,10},{3,11},{4,12},{5,13},{6,14},{7,15},{8,0},{9,1},... | collective-permute-start | bytes 442376 | tf_op jit(solution)/shard_map/ppermute | solution.py:288
  3.1 11.4 %collective-permute-start.1 = (bf16[144,512]{1,0:T(8,128)(2,1)S(1)}, bf16[144,512]{1,0:T(8,128)(2,1)S(1)}, u32[]{:S(2)}, u32[]{:S(2)}) collective-permute-start(bf16[144,512]{1,0:T(8,128)(2,1)S(1)} %gather.1.refs_0_.refs_1_), channel_id=1, source_target_pairs={{0,4},{1,5},{2,6},{3,7},{4,0},{5,1},{6,2},{7,3},{8,12},{9,13},{10,... | collective-permute-start | bytes 442376 | tf_op jit(solution)/shard_map/ppermute | solution.py:288
  6.8 7.9 %collective-permute-start.4 = (bf16[144,512]{1,0:T(8,128)(2,1)S(1)}, bf16[144,512]{1,0:T(8,128)(2,1)S(1)}, u32[]{:S(2)}, u32[]{:S(2)}) collective-permute-start(bf16[144,512]{1,0:T(8,128)(2,1)S(1)} %gather.1.refs_0_.refs_1_), channel_id=1, source_target_pairs={{0,2},{1,3},{2,0},{3,1},{4,6},{5,7},{6,4},{7,5},{8,10},{9,11},{10,... | collective-permute-start | bytes 442376 | tf_op jit(solution)/shard_map/ppermute | solution.py:288
  8.3 6.3 %collective-permute-start.3 = (bf16[144,512]{1,0:T(8,128)(2,1)S(1)}, bf16[144,512]{1,0:T(8,128)(2,1)S(1)}, u32[]{:S(2)}, u32[]{:S(2)}) collective-permute-start(bf16[144,512]{1,0:T(8,128)(2,1)S(1)} %gather.1.refs_0_.refs_1_), channel_id=1, source_target_pairs={{0,16},{1,17},{2,18},{3,19},{4,20},{5,21},{6,22},{7,23},{8,9},{9,8... | collective-permute-start | bytes 442376 | tf_op jit(solution)/shard_map/ppermute | solution.py:288
  14.7 4.8 %collective-permute-start.5 = (bf16[432,512]{1,0:T(8,128)(2,1)S(1)}, bf16[432,512]{1,0:T(8,128)(2,1)S(1)}, u32[]{:S(2)}, u32[]{:S(2)}) collective-permute-start(bf16[432,512]{1,0:T(8,128)(2,1)S(1)} %joined.12), channel_id=1, source_target_pairs={{0,8},{1,9},{2,10},{3,11},{4,12},{5,13},{6,14},{7,15},{8,0},{9,1},... | collective-permute-start | bytes 1327112 | tf_op jit(solution)/shard_map/ppermute | solution.py:288
  14.8 10.1 %collective-permute-start.7 = (bf16[288,512]{1,0:T(8,128)(2,1)S(1)}, bf16[288,512]{1,0:T(8,128)(2,1)S(1)}, u32[]{:S(2)}, u32[]{:S(2)}) collective-permute-start(bf16[288,512]{1,0:T(8,128)(2,1)S(1)} %joined.14.refs_0_.refs_1_), channel_id=1, source_target_pairs={{0,16},{1,17},{2,18},{3,19},{4,20},{5,21},{6,22},{7,23},{8,9},{9,8... | collective-permute-start | bytes 884744 | tf_op jit(solution)/shard_map/ppermute | solution.py:288
  16.4 9.8 %collective-permute-start.6 = (bf16[288,512]{1,0:T(8,128)(2,1)S(1)}, bf16[288,512]{1,0:T(8,128)(2,1)S(1)}, u32[]{:S(2)}, u32[]{:S(2)}) collective-permute-start(bf16[288,512]{1,0:T(8,128)(2,1)S(1)} %joined.15), channel_id=1, source_target_pairs={{0,1},{1,0},{2,3},{3,2},{4,5},{5,4},{6,7},{7,6},{8,24},{9,25},{10,... | collective-permute-start | bytes 884744 | tf_op jit(solution)/shard_map/ppermute | solution.py:288
  18.0 6.2 %collective-permute-start.2 = (bf16[144,512]{1,0:T(8,128)(2,1)S(1)}, bf16[144,512]{1,0:T(8,128)(2,1)S(1)}, u32[]{:S(2)}, u32[]{:S(2)}) collective-permute-start(bf16[144,512]{1,0:T(8,128)(2,1)S(1)} %joined.11.refs_0_), channel_id=1, source_target_pairs={{0,2},{1,3},{2,0},{3,1},{4,6},{5,7},{6,4},{7,5},{8,10},{9,11},{10,... | collective-permute-start | bytes 442376 | tf_op jit(solution)/shard_map/ppermute | solution.py:288
  24.3 6.8 %collective-permute-start.9 = (bf16[144,512]{1,0:T(8,128)(2,1)S(1)}, bf16[144,512]{1,0:T(8,128)(2,1)S(1)}, u32[]{:S(2)}, u32[]{:S(2)}) collective-permute-start(bf16[144,512]{1,0:T(8,128)(2,1)S(1)} %joined.13.refs_0_), channel_id=1, source_target_pairs={{0,16},{1,17},{2,18},{3,19},{4,20},{5,21},{6,22},{7,23},{8,9},{9,8... | collective-permute-start | bytes 442376 | tf_op jit(solution)/shard_map/ppermute | solution.py:288
  24.9 13.7 %collective-permute-start.11 = (bf16[576,512]{1,0:T(8,128)(2,1)S(1)}, bf16[576,512]{1,0:T(8,128)(2,1)S(1)}, u32[]{:S(2)}, u32[]{:S(2)}) collective-permute-start(bf16[576,512]{1,0:T(8,128)(2,1)S(1)} %joined.18), channel_id=1, source_target_pairs={{0,1},{1,0},{2,3},{3,2},{4,5},{5,4},{6,7},{7,6},{8,24},{9,25},{10,... | collective-permute-start | bytes 1769480 | tf_op jit(solution)/shard_map/ppermute | solution.py:288
  26.3 6.2 %collective-permute-start.8 = (bf16[720,512]{1,0:T(8,128)(2,1)S(1)}, bf16[720,512]{1,0:T(8,128)(2,1)S(1)}, u32[]{:S(2)}, u32[]{:S(2)}) collective-permute-start(bf16[720,512]{1,0:T(8,128)(2,1)S(1)} %joined.16), channel_id=1, source_target_pairs={{0,8},{1,9},{2,10},{3,11},{4,12},{5,13},{6,14},{7,15},{8,0},{9,1},... | collective-permute-start | bytes 2211848 | tf_op jit(solution)/shard_map/ppermute | solution.py:288
  31.1 1.4 %collective-permute-start.10 = (bf16[144,512]{1,0:T(8,128)(2,1)S(1)}, bf16[144,512]{1,0:T(8,128)(2,1)S(1)}, u32[]{:S(2)}, u32[]{:S(2)}) collective-permute-start(bf16[144,512]{1,0:T(8,128)(2,1)S(1)} %joined.17), channel_id=1, source_target_pairs={{0,8},{1,9},{2,10},{3,11},{4,12},{5,13},{6,14},{7,15},{8,0},{9,1},... | collective-permute-start | bytes 442376 | tf_op jit(solution)/shard_map/ppermute | solution.py:288
  31.2 7.8 %collective-permute-start.13 = (bf16[288,512]{1,0:T(8,128)(2,1)S(1)}, bf16[288,512]{1,0:T(8,128)(2,1)S(1)}, u32[]{:S(2)}, u32[]{:S(2)}) collective-permute-start(bf16[288,512]{1,0:T(8,128)(2,1)S(1)} %joined.20), channel_id=1, source_target_pairs={{0,1},{1,0},{2,3},{3,2},{4,5},{5,4},{6,7},{7,6},{8,24},{9,25},{10,... | collective-permute-start | bytes 884744 | tf_op jit(solution)/shard_map/ppermute | solution.py:288
  38.7 5.3 %collective-permute-start.12 = (bf16[576,512]{1,0:T(8,128)(2,1)S(1)}, bf16[576,512]{1,0:T(8,128)(2,1)S(1)}, u32[]{:S(2)}, u32[]{:S(2)}) collective-permute-start(bf16[576,512]{1,0:T(8,128)(2,1)S(1)} %joined.19), channel_id=1, source_target_pairs={{0,8},{1,9},{2,10},{3,11},{4,12},{5,13},{6,14},{7,15},{8,0},{9,1},... | collective-permute-start | bytes 1769480 | tf_op jit(solution)/shard_map/ppermute | solution.py:288
  38.9 5.1 %collective-permute-start.14 = (bf16[288,512]{1,0:T(8,128)(2,1)S(1)}, bf16[288,512]{1,0:T(8,128)(2,1)S(1)}, u32[]{:S(2)}, u32[]{:S(2)}) collective-permute-start(bf16[288,512]{1,0:T(8,128)(2,1)S(1)} %joined.21), channel_id=1, source_target_pairs={{0,8},{1,9},{2,10},{3,11},{4,12},{5,13},{6,14},{7,15},{8,0},{9,1},... | collective-permute-start | bytes 884744 | tf_op jit(solution)/shard_map/ppermute | solution.py:288
  39.4 4.7 %copy-start = (f32[2048]{0:T(1024)S(1)}, f32[2048]{0:T(1024)}, u32[]{:S(2)}) copy-start(f32[2048]{0:T(1024)} %param.9) | copy-start | bytes 24580

commit v5 on v4

--- a/solution.py
+++ b/solution.py
@@ -12,7 +12,7 @@
 AXES = ("blk", "grp")
 EXTRA = 16
 LANES = 128
-OUT = 256
+OUT = 128
 VMEM = pl.BlockSpec(memory_space=pltpu.VMEM)
 NT = (((1,), (1,)), ((), ()))
 

time: 50.4 us -> 50.4 us (level)
  no operation moved by 1% of the time
where the time goes in v5:
time: 50.4 us; the launch traced here: 50.3 us
  Pallas kernels  30.2 us (60%)
  starting transfers between devices  15.2 us (30%)
  waiting for transfers between devices  3.83 us (8%)
  between operations  0.97 us (2%)
    pallas_call x6, Pallas kernels, visit(): pl.pallas_call(functools.partial(visit_kernel, len(shards), count, block,...  28 us
    ppermute x15, starting transfers between devices, swap(): return lax.ppermute(array, AXES, route)  15.2 us
    ppermute x15, waiting for transfers between devices, swap(): return lax.ppermute(array, AXES, route)  3.83 us
    pallas_call x1, Pallas kernels, gather(): pl.pallas_call(gather_kernel, out_shape=pltpu.VMEM((count + EXTRA, width)...  1.94 us
  transfers between devices with their start and end apart: 15, of which 4 were waited for; matrix products, arithmetic and copies ran while one was open for 0% of the time, Pallas kernels for 44%

profile of v5, /device:TPU:0, one launch (start us, length us, event | category | flops | bytes accessed | tf_op | source)
XLA Modules:
  0.0 50.3 jit_solution(8692941735262036443)
XLA Ops:
  0.6 1.9 %gather.1.refs_0_.refs_1_ = bf16[144,512]{1,0:T(8,128)(2,1)S(1)} custom-call(bf16[2048,512]{1,0:T(8,128)(2,1)} %table_ref.1, s32[1,128]{1,0:T(1,128)} %bitcast.5, bf16[1,128]{1,0:T(2,128)(2,1)} %bitcast.6), custom_call_target="tpu_custom_call" | custom-call | tf_op jit(solution)/shard_map/gather/pallas_call | solution.py:70
  2.6 0.5 %collective-permute-start = (bf16[144,512]{1,0:T(8,128)(2,1)S(1)}, bf16[144,512]{1,0:T(8,128)(2,1)S(1)}, u32[]{:S(2)}, u32[]{:S(2)}) collective-permute-start(bf16[144,512]{1,0:T(8,128)(2,1)S(1)} %gather.1.refs_0_.refs_1_), channel_id=1, source_target_pairs={{0,8},{1,9},{2,10},{3,11},{4,12},{5,13},{6,14},{7,15},{8,0},{9,1},... | collective-permute-start | bytes 442376 | tf_op jit(solution)/shard_map/ppermute | solution.py:288
  3.1 3.7 %collective-permute-start.1 = (bf16[144,512]{1,0:T(8,128)(2,1)S(1)}, bf16[144,512]{1,0:T(8,128)(2,1)S(1)}, u32[]{:S(2)}, u32[]{:S(2)}) collective-permute-start(bf16[144,512]{1,0:T(8,128)(2,1)S(1)} %gather.1.refs_0_.refs_1_), channel_id=1, source_target_pairs={{0,4},{1,5},{2,6},{3,7},{4,0},{5,1},{6,2},{7,3},{8,12},{9,13},{10,... | collective-permute-start | bytes 442376 | tf_op jit(solution)/shard_map/ppermute | solution.py:288
  6.8 1.6 %collective-permute-start.4 = (bf16[144,512]{1,0:T(8,128)(2,1)S(1)}, bf16[144,512]{1,0:T(8,128)(2,1)S(1)}, u32[]{:S(2)}, u32[]{:S(2)}) collective-permute-start(bf16[144,512]{1,0:T(8,128)(2,1)S(1)} %gather.1.refs_0_.refs_1_), channel_id=1, source_target_pairs={{0,2},{1,3},{2,0},{3,1},{4,6},{5,7},{6,4},{7,5},{8,10},{9,11},{10,... | collective-permute-start | bytes 442376 | tf_op jit(solution)/shard_map/ppermute | solution.py:288
  8.3 1.5 %collective-permute-start.3 = (bf16[144,512]{1,0:T(8,128)(2,1)S(1)}, bf16[144,512]{1,0:T(8,128)(2,1)S(1)}, u32[]{:S(2)}, u32[]{:S(2)}) collective-permute-start(bf16[144,512]{1,0:T(8,128)(2,1)S(1)} %gather.1.refs_0_.refs_1_), channel_id=1, source_target_pairs={{0,16},{1,17},{2,18},{3,19},{4,20},{5,21},{6,22},{7,23},{8,9},{9,8... | collective-permute-start | bytes 442376 | tf_op jit(solution)/shard_map/ppermute | solution.py:288
  9.8 0.0 collective-permute-done.refs_1_
  9.8 3.1 %visit.6 = (f32[2048,128]{1,0:T(8,128)S(1)}, f32[2048,128]{1,0:T(8,128)S(1)}, f32[2048,512]{1,0:T(8,128)S(1)}, f32[8,128]{1,0:T(8,128)S(1)}, f32[16,128]{1,0:T(8,128)S(1)}, /*index=5*/bf16[2048,512]{1,0:T(8,128)(2,1)S(1)}) custom-call(bf16[144,512]{1,0:T(8,128)(2,1)S(1)} %gather.1.refs_0_.refs_1_, bf16[144,512]{1,0:T(8,128)(2,1)S(1)} %collective-permute-done.refs_1_, ...), custom_call_target="tpu_custom_call" | custom-call | flops 10737418 | bytes 1024 | tf_op jit(solution)/shard_map/visit/pallas_call | solution.py:244
  12.9 1.5 %collective-permute-done.1.refs_1_.refs_3_.refs_2_ = bf16[144,512]{1,0:T(8,128)(2,1)S(1)} collective-permute-done((bf16[144,512]{1,0:T(8,128)(2,1)S(1)}, bf16[144,512]{1,0:T(8,128)(2,1)S(1)}, u32[]{:S(2)}, u32[]{:S(2)}) %collective-permute-start.1) | collective-permute-done | bytes 147488 | tf_op jit(solution)/shard_map/ppermute | solution.py:288
  14.5 0.2 collective-permute-done.4.refs_2_.refs_1_
  14.7 0.0 collective-permute-done.3.refs_1_.refs_0_.refs_2_
  14.7 0.1 collective-permute-start.5
  14.8 1.6 %collective-permute-start.7 = (bf16[288,512]{1,0:T(8,128)(2,1)S(1)}, bf16[288,512]{1,0:T(8,128)(2,1)S(1)}, u32[]{:S(2)}, u32[]{:S(2)}) collective-permute-start(bf16[288,512]{1,0:T(8,128)(2,1)S(1)} %joined.14.refs_0_.refs_1_), channel_id=1, source_target_pairs={{0,16},{1,17},{2,18},{3,19},{4,20},{5,21},{6,22},{7,23},{8,9},{9,8... | collective-permute-start | bytes 884744 | tf_op jit(solution)/shard_map/ppermute | solution.py:288
  16.4 1.6 %collective-permute-start.6 = (bf16[288,512]{1,0:T(8,128)(2,1)S(1)}, bf16[288,512]{1,0:T(8,128)(2,1)S(1)}, u32[]{:S(2)}, u32[]{:S(2)}) collective-permute-start(bf16[288,512]{1,0:T(8,128)(2,1)S(1)} %joined.15), channel_id=1, source_target_pairs={{0,1},{1,0},{2,3},{3,2},{4,5},{5,4},{6,7},{7,6},{8,24},{9,25},{10,... | collective-permute-start | bytes 884744 | tf_op jit(solution)/shard_map/ppermute | solution.py:288
  18.0 1.4 %collective-permute-start.2 = (bf16[144,512]{1,0:T(8,128)(2,1)S(1)}, bf16[144,512]{1,0:T(8,128)(2,1)S(1)}, u32[]{:S(2)}, u32[]{:S(2)}) collective-permute-start(bf16[144,512]{1,0:T(8,128)(2,1)S(1)} %joined.11.refs_0_), channel_id=1, source_target_pairs={{0,2},{1,3},{2,0},{3,1},{4,6},{5,7},{6,4},{7,5},{8,10},{9,11},{10,... | collective-permute-start | bytes 442376 | tf_op jit(solution)/shard_map/ppermute | solution.py:288
  19.5 0.0 collective-permute-done.5.refs_3_
  19.5 4.7 %visit.7 = (f32[2048,128]{1,0:T(8,128)S(1)}, f32[2048,128]{1,0:T(8,128)S(1)}, f32[2048,512]{1,0:T(8,128)S(1)}, f32[8,128]{1,0:T(8,128)S(1)}) custom-call(bf16[144,512]{1,0:T(8,128)(2,1)S(1)} %collective-permute-done.3.refs_1_.refs_0_.refs_2_, ...), custom_call_target="tpu_custom_call", output_to_operand_aliasing={{0}: (5, {}), {1}: (6, {}), {2}: (7, {})} | custom-call | flops 322122560 | bytes 1024 | tf_op jit(solution)/shard_map/visit/pallas_call | solution.py:244
  24.2 0.0 collective-permute-done.2.refs_1_.refs_3_.refs_0_
  24.3 0.6 %collective-permute-start.9 = (bf16[144,512]{1,0:T(8,128)(2,1)S(1)}, bf16[144,512]{1,0:T(8,128)(2,1)S(1)}, u32[]{:S(2)}, u32[]{:S(2)}) collective-permute-start(bf16[144,512]{1,0:T(8,128)(2,1)S(1)} %joined.13.refs_0_), channel_id=1, source_target_pairs={{0,16},{1,17},{2,18},{3,19},{4,20},{5,21},{6,22},{7,23},{8,9},{9,8... | collective-permute-start | bytes 442376 | tf_op jit(solution)/shard_map/ppermute | solution.py:288
  24.9 0.0 collective-permute-done.7.refs_2_.refs_1_
  24.9 1.3 %collective-permute-start.11 = (bf16[576,512]{1,0:T(8,128)(2,1)S(1)}, bf16[576,512]{1,0:T(8,128)(2,1)S(1)}, u32[]{:S(2)}, u32[]{:S(2)}) collective-permute-start(bf16[576,512]{1,0:T(8,128)(2,1)S(1)} %joined.18), channel_id=1, source_target_pairs={{0,1},{1,0},{2,3},{3,2},{4,5},{5,4},{6,7},{7,6},{8,24},{9,25},{10,... | collective-permute-start | bytes 1769480 | tf_op jit(solution)/shard_map/ppermute | solution.py:288
  26.2 0.0 collective-permute-done.6.refs_1_.refs_0_
  26.3 0.1 collective-permute-start.8
  26.4 3.4 %visit.8 = (f32[2048,128]{1,0:T(8,128)S(1)}, f32[2048,128]{1,0:T(8,128)S(1)}, f32[2048,512]{1,0:T(8,128)S(1)}, f32[8,128]{1,0:T(8,128)S(1)}) custom-call(bf16[288,512]{1,0:T(8,128)(2,1)S(1)} %collective-permute-done.6.refs_1_.refs_0_, ...), custom_call_target="tpu_custom_call", output_to_operand_aliasing={{0}: (3, {}), {1}: (4, {}), {2}: (5, {})} | custom-call | flops 6442450944 | bytes 1024 | tf_op jit(solution)/shard_map/visit/pallas_call | solution.py:244
  29.7 1.3 %collective-permute-done.9.refs_1_.refs_2_ = bf16[144,512]{1,0:T(8,128)(2,1)S(1)} collective-permute-done((bf16[144,512]{1,0:T(8,128)(2,1)S(1)}, bf16[144,512]{1,0:T(8,128)(2,1)S(1)}, u32[]{:S(2)}, u32[]{:S(2)}) %collective-permute-start.9) | collective-permute-done | bytes 147488 | tf_op jit(solution)/shard_map/ppermute | solution.py:288
  31.1 0.1 collective-permute-start.10
  31.2 0.6 %collective-permute-start.13 = (bf16[288,512]{1,0:T(8,128)(2,1)S(1)}, bf16[288,512]{1,0:T(8,128)(2,1)S(1)}, u32[]{:S(2)}, u32[]{:S(2)}) collective-permute-start(bf16[288,512]{1,0:T(8,128)(2,1)S(1)} %joined.20), channel_id=1, source_target_pairs={{0,1},{1,0},{2,3},{3,2},{4,5},{5,4},{6,7},{7,6},{8,24},{9,25},{10,... | collective-permute-start | bytes 884744 | tf_op jit(solution)/shard_map/ppermute | solution.py:288
  31.7 0.8 %collective-permute-done.10.refs_3_ = bf16[144,512]{1,0:T(8,128)(2,1)S(1)} collective-permute-done((bf16[144,512]{1,0:T(8,128)(2,1)S(1)}, bf16[144,512]{1,0:T(8,128)(2,1)S(1)}, u32[]{:S(2)}, u32[]{:S(2)}) %collective-permute-start.10) | collective-permute-done | bytes 147488 | tf_op jit(solution)/shard_map/ppermute | solution.py:288
  32.5 0.0 collective-permute-done.8.refs_1_
  32.5 6.1 %visit.9 = (f32[2048,128]{1,0:T(8,128)S(1)}, f32[2048,128]{1,0:T(8,128)S(1)}, f32[2048,512]{1,0:T(8,128)S(1)}, f32[8,128]{1,0:T(8,128)S(1)}) custom-call(bf16[144,512]{1,0:T(8,128)(2,1)S(1)} %collective-permute-done.2.refs_1_.refs_3_.refs_0_, ...), custom_call_target="tpu_custom_call", output_to_operand_aliasing={{0}: (5, {}), {1}: (6, {}), {2}: (7, {})} | custom-call | flops 1717986944 | bytes 1024 | tf_op jit(solution)/shard_map/visit/pallas_call | solution.py:244
  38.6 0.0 collective-permute-done.11.refs_1_.refs_0_
  38.7 0.2 collective-permute-start.12
  38.9 0.0 collective-permute-done.13.refs_1_
  38.9 0.4 collective-permute-start.14
  39.4 0.0 copy-start
  39.4 4.6 %visit.10 = (f32[2048,128]{1,0:T(8,128)S(1)}, f32[2048,128]{1,0:T(8,128)S(1)}, f32[2048,512]{1,0:T(8,128)S(1)}, f32[8,128]{1,0:T(8,128)}) custom-call(bf16[576,512]{1,0:T(8,128)(2,1)S(1)} %collective-permute-done.11.refs_1_.refs_0_, bf16[288,512]{1,0:T(8,128)(2,1)S(1)} %collective-permute-done.13.refs_1_, ...), custom_call_target="tpu_custom_call", output_to_operand_aliasing={{0}: (3, {}), {1}: (4, {}), {2}: (5, {})} | custom-call | flops 3221225472 | bytes 1024 | tf_op jit(solution)/shard_map/visit/pallas_call | solution.py:244
  44.0 0.0 collective-permute-done.14.refs_1_
  44.0 0.0 collective-permute-done.12.refs_0_
  44.0 0.0 copy-done
  44.1 6.0 %visit.11 = (f32[2048,512]{1,0:T(8,128)}, f32[16,128]{1,0:T(8,128)}) custom-call(bf16[576,512]{1,0:T(8,128)(2,1)S(1)} %collective-permute-done.12.refs_0_, bf16[288,512]{1,0:T(8,128)(2,1)S(1)} %collective-permute-done.14.refs_1_, bf16[2048,512]{1,0:T(8,128)(2,1)S(1)} %get-tuple-element.26.refs_4_.refs_2_, f32[2048,128]{1,0:T(8,128)S(1)} %get-tuple-element.42.refs_3_, ...), custom_call_target="tpu_custom_call" | custom-call | flops 3221225472 | bytes 1024 | tf_op jit(solution)/shard_map/visit/pallas_call | solution.py:244
  (11 shorter events, 0.3 us)
Async XLA Ops:
  2.6 7.3 %collective-permute-start = (bf16[144,512]{1,0:T(8,128)(2,1)S(1)}, bf16[144,512]{1,0:T(8,128)(2,1)S(1)}, u32[]{:S(2)}, u32[]{:S(2)}) collective-permute-start(bf16[144,512]{1,0:T(8,128)(2,1)S(1)} %gather.1.refs_0_.refs_1_), channel_id=1, source_target_pairs={{0,8},{1,9},{2,10},{3,11},{4,12},{5,13},{6,14},{7,15},{8,0},{9,1},... | collective-permute-start | bytes 442376 | tf_op jit(solution)/shard_map/ppermute | solution.py:288
  3.1 11.4 %collective-permute-start.1 = (bf16[144,512]{1,0:T(8,128)(2,1)S(1)}, bf16[144,512]{1,0:T(8,128)(2,1)S(1)}, u32[]{:S(2)}, u32[]{:S(2)}) collective-permute-start(bf16[144,512]{1,0:T(8,128)(2,1)S(1)} %gather.1.refs_0_.refs_1_), channel_id=1, source_target_pairs={{0,4},{1,5},{2,6},{3,7},{4,0},{5,1},{6,2},{7,3},{8,12},{9,13},{10,... | collective-permute-start | bytes 442376 | tf_op jit(solution)/shard_map/ppermute | solution.py:288
  6.8 7.9 %collective-permute-start.4 = (bf16[144,512]{1,0:T(8,128)(2,1)S(1)}, bf16[144,512]{1,0:T(8,128)(2,1)S(1)}, u32[]{:S(2)}, u32[]{:S(2)}) collective-permute-start(bf16[144,512]{1,0:T(8,128)(2,1)S(1)} %gather.1.refs_0_.refs_1_), channel_id=1, source_target_pairs={{0,2},{1,3},{2,0},{3,1},{4,6},{5,7},{6,4},{7,5},{8,10},{9,11},{10,... | collective-permute-start | bytes 442376 | tf_op jit(solution)/shard_map/ppermute | solution.py:288
  8.3 6.3 %collective-permute-start.3 = (bf16[144,512]{1,0:T(8,128)(2,1)S(1)}, bf16[144,512]{1,0:T(8,128)(2,1)S(1)}, u32[]{:S(2)}, u32[]{:S(2)}) collective-permute-start(bf16[144,512]{1,0:T(8,128)(2,1)S(1)} %gather.1.refs_0_.refs_1_), channel_id=1, source_target_pairs={{0,16},{1,17},{2,18},{3,19},{4,20},{5,21},{6,22},{7,23},{8,9},{9,8... | collective-permute-start | bytes 442376 | tf_op jit(solution)/shard_map/ppermute | solution.py:288
  14.7 4.8 %collective-permute-start.5 = (bf16[432,512]{1,0:T(8,128)(2,1)S(1)}, bf16[432,512]{1,0:T(8,128)(2,1)S(1)}, u32[]{:S(2)}, u32[]{:S(2)}) collective-permute-start(bf16[432,512]{1,0:T(8,128)(2,1)S(1)} %joined.12), channel_id=1, source_target_pairs={{0,8},{1,9},{2,10},{3,11},{4,12},{5,13},{6,14},{7,15},{8,0},{9,1},... | collective-permute-start | bytes 1327112 | tf_op jit(solution)/shard_map/ppermute | solution.py:288
  14.8 10.1 %collective-permute-start.7 = (bf16[288,512]{1,0:T(8,128)(2,1)S(1)}, bf16[288,512]{1,0:T(8,128)(2,1)S(1)}, u32[]{:S(2)}, u32[]{:S(2)}) collective-permute-start(bf16[288,512]{1,0:T(8,128)(2,1)S(1)} %joined.14.refs_0_.refs_1_), channel_id=1, source_target_pairs={{0,16},{1,17},{2,18},{3,19},{4,20},{5,21},{6,22},{7,23},{8,9},{9,8... | collective-permute-start | bytes 884744 | tf_op jit(solution)/shard_map/ppermute | solution.py:288
  16.4 9.8 %collective-permute-start.6 = (bf16[288,512]{1,0:T(8,128)(2,1)S(1)}, bf16[288,512]{1,0:T(8,128)(2,1)S(1)}, u32[]{:S(2)}, u32[]{:S(2)}) collective-permute-start(bf16[288,512]{1,0:T(8,128)(2,1)S(1)} %joined.15), channel_id=1, source_target_pairs={{0,1},{1,0},{2,3},{3,2},{4,5},{5,4},{6,7},{7,6},{8,24},{9,25},{10,... | collective-permute-start | bytes 884744 | tf_op jit(solution)/shard_map/ppermute | solution.py:288
  18.0 6.2 %collective-permute-start.2 = (bf16[144,512]{1,0:T(8,128)(2,1)S(1)}, bf16[144,512]{1,0:T(8,128)(2,1)S(1)}, u32[]{:S(2)}, u32[]{:S(2)}) collective-permute-start(bf16[144,512]{1,0:T(8,128)(2,1)S(1)} %joined.11.refs_0_), channel_id=1, source_target_pairs={{0,2},{1,3},{2,0},{3,1},{4,6},{5,7},{6,4},{7,5},{8,10},{9,11},{10,... | collective-permute-start | bytes 442376 | tf_op jit(solution)/shard_map/ppermute | solution.py:288
  24.3 6.8 %collective-permute-start.9 = (bf16[144,512]{1,0:T(8,128)(2,1)S(1)}, bf16[144,512]{1,0:T(8,128)(2,1)S(1)}, u32[]{:S(2)}, u32[]{:S(2)}) collective-permute-start(bf16[144,512]{1,0:T(8,128)(2,1)S(1)} %joined.13.refs_0_), channel_id=1, source_target_pairs={{0,16},{1,17},{2,18},{3,19},{4,20},{5,21},{6,22},{7,23},{8,9},{9,8... | collective-permute-start | bytes 442376 | tf_op jit(solution)/shard_map/ppermute | solution.py:288
  24.9 13.7 %collective-permute-start.11 = (bf16[576,512]{1,0:T(8,128)(2,1)S(1)}, bf16[576,512]{1,0:T(8,128)(2,1)S(1)}, u32[]{:S(2)}, u32[]{:S(2)}) collective-permute-start(bf16[576,512]{1,0:T(8,128)(2,1)S(1)} %joined.18), channel_id=1, source_target_pairs={{0,1},{1,0},{2,3},{3,2},{4,5},{5,4},{6,7},{7,6},{8,24},{9,25},{10,... | collective-permute-start | bytes 1769480 | tf_op jit(solution)/shard_map/ppermute | solution.py:288
  26.3 6.2 %collective-permute-start.8 = (bf16[720,512]{1,0:T(8,128)(2,1)S(1)}, bf16[720,512]{1,0:T(8,128)(2,1)S(1)}, u32[]{:S(2)}, u32[]{:S(2)}) collective-permute-start(bf16[720,512]{1,0:T(8,128)(2,1)S(1)} %joined.16), channel_id=1, source_target_pairs={{0,8},{1,9},{2,10},{3,11},{4,12},{5,13},{6,14},{7,15},{8,0},{9,1},... | collective-permute-start | bytes 2211848 | tf_op jit(solution)/shard_map/ppermute | solution.py:288
  31.1 1.4 %collective-permute-start.10 = (bf16[144,512]{1,0:T(8,128)(2,1)S(1)}, bf16[144,512]{1,0:T(8,128)(2,1)S(1)}, u32[]{:S(2)}, u32[]{:S(2)}) collective-permute-start(bf16[144,512]{1,0:T(8,128)(2,1)S(1)} %joined.17), channel_id=1, source_target_pairs={{0,8},{1,9},{2,10},{3,11},{4,12},{5,13},{6,14},{7,15},{8,0},{9,1},... | collective-permute-start | bytes 442376 | tf_op jit(solution)/shard_map/ppermute | solution.py:288
  31.2 7.8 %collective-permute-start.13 = (bf16[288,512]{1,0:T(8,128)(2,1)S(1)}, bf16[288,512]{1,0:T(8,128)(2,1)S(1)}, u32[]{:S(2)}, u32[]{:S(2)}) collective-permute-start(bf16[288,512]{1,0:T(8,128)(2,1)S(1)} %joined.20), channel_id=1, source_target_pairs={{0,1},{1,0},{2,3},{3,2},{4,5},{5,4},{6,7},{7,6},{8,24},{9,25},{10,... | collective-permute-start | bytes 884744 | tf_op jit(solution)/shard_map/ppermute | solution.py:288
  38.7 5.3 %collective-permute-start.12 = (bf16[576,512]{1,0:T(8,128)(2,1)S(1)}, bf16[576,512]{1,0:T(8,128)(2,1)S(1)}, u32[]{:S(2)}, u32[]{:S(2)}) collective-permute-start(bf16[576,512]{1,0:T(8,128)(2,1)S(1)} %joined.19), channel_id=1, source_target_pairs={{0,8},{1,9},{2,10},{3,11},{4,12},{5,13},{6,14},{7,15},{8,0},{9,1},... | collective-permute-start | bytes 1769480 | tf_op jit(solution)/shard_map/ppermute | solution.py:288
  38.9 5.1 %collective-permute-start.14 = (bf16[288,512]{1,0:T(8,128)(2,1)S(1)}, bf16[288,512]{1,0:T(8,128)(2,1)S(1)}, u32[]{:S(2)}, u32[]{:S(2)}) collective-permute-start(bf16[288,512]{1,0:T(8,128)(2,1)S(1)} %joined.21), channel_id=1, source_target_pairs={{0,8},{1,9},{2,10},{3,11},{4,12},{5,13},{6,14},{7,15},{8,0},{9,1},... | collective-permute-start | bytes 884744 | tf_op jit(solution)/shard_map/ppermute | solution.py:288
  39.4 4.7 %copy-start = (f32[2048]{0:T(1024)S(1)}, f32[2048]{0:T(1024)}, u32[]{:S(2)}) copy-start(f32[2048]{0:T(1024)} %param.9) | copy-start | bytes 24580
